TPU v7x, 256 devices: a whole 4x4x8 slice. The times are simulated.
256 devices in a mesh: gx: 32 (over z_lo, x, core), gy: 8 (over y, z_hi).
Axes of the slice: x: 4, y: 4, z: 8 (z_hi: 2, z_lo: 4; z = z_hi * 4 + z_lo), core: 2. Of those that a mesh axis runs over, the one named last changes fastest.
Arguments:
- saved_queries: bfloat16 [128, 64, 16, 128], P('gx', 'gy'), may hold values from -24 to 24
- saved_keys: bfloat16 [4, 128, 64, 16, 128], P(None, 'gx', 'gy'), may hold values from -4.5 to 4.5
- saved_values: bfloat16 [4, 128, 64, 16, 128], P(None, 'gx', 'gy'), may hold values from -4.5 to 4.5
- out_grad: bfloat16 [128, 64, 16, 128], P('gx', 'gy'), may hold values from -4.5 to 4.5
- shifts: int32 [3, 2], replicated, may hold values from -1 to 1, as said below
Outputs:
- d_queries: bfloat16 [128, 64, 16, 128], P('gx', 'gy')
- d_keys: bfloat16 [4, 128, 64, 16, 128], P(None, 'gx', 'gy')
- d_values: bfloat16 [4, 128, 64, 16, 128], P(None, 'gx', 'gy')
Inputs may be any that keep to these rules, and one draw needn't show every extreme that they name: `shifts`: at least one entry has magnitude 1.
All inputs are finite; a program needn't handle non-finite values.
Results may differ from a plain program's by a relative error of at most 0.0095.
Values may be sent and summed in bfloat16 or wider, within the bound.
A program may use at most 128 MiB of HBM per device.

v0:
```python
import math

import jax
import jax.numpy as jnp
import numpy as np
from jax import lax
from jax.sharding import PartitionSpec as P

HEADS = 4
HD = 32
SMAX = 1
BLOCK_Y = 8
BLOCK_Z = 4


def passed_along(shard, axis, by):
    peers = lax.axis_size(axis)
    pairs = [(i, i + by) for i in range(peers) if 0 <= i + by < peers]
    return lax.ppermute(shard, axis, pairs)


def with_halo(block, sides, width):
    for axis, dim in sides:
        count = lax.axis_size(axis)
        forward = [(i, i + 1) for i in range(count - 1)]
        backward = [(target, source) for source, target in forward]
        low = lax.ppermute(
            lax.slice_in_dim(block, block.shape[dim] - width, None, axis=dim), axis, forward
        )
        high = lax.ppermute(lax.slice_in_dim(block, 0, width, axis=dim), axis, backward)
        block = jnp.concatenate([low, block, high], axis=dim)
    return block


def window_table(rows_x, span_y, span_z):
    query_ids = np.arange(rows_x * span_y * span_z)
    query_x = query_ids // (span_y * span_z)
    query_y = query_ids // span_z % span_y
    query_z = query_ids % span_z
    region_ids = np.arange((rows_x + 4) * (span_y + 4) * (span_z + 2))
    region_x = region_ids // ((span_y + 4) * (span_z + 2))
    region_y = region_ids // (span_z + 2) % (span_y + 4)
    region_z = region_ids % (span_z + 2)
    gap_x = region_x[None, :] - query_x[:, None]
    gap_y = region_y[None, :] - query_y[:, None]
    gap_z = region_z[None, :] - query_z[:, None]
    table = (gap_x >= 0) & (gap_x <= 4) & (gap_y >= 0) & (gap_y <= 4) & (gap_z >= 0) & (gap_z <= 2)
    return jnp.asarray(table)


def fold_rows(acc_keys, acc_values, halo_reach):
    inner = acc_keys.shape[1] - 2 * halo_reach
    low_rims = jnp.stack([acc_keys[:, :halo_reach], acc_values[:, :halo_reach]])
    high_rims = jnp.stack([acc_keys[:, inner + halo_reach :], acc_values[:, inner + halo_reach :]])
    from_next = passed_along(low_rims.astype(jnp.bfloat16), "gx", -1).astype(low_rims.dtype)
    from_prev = passed_along(high_rims.astype(jnp.bfloat16), "gx", 1).astype(high_rims.dtype)
    core_keys = acc_keys[:, halo_reach : halo_reach + inner]
    core_keys = (
        core_keys.at[:, :halo_reach].add(from_prev[0]).at[:, inner - halo_reach :].add(from_next[0])
    )
    core_values = acc_values[:, halo_reach : halo_reach + inner]
    core_values = (
        core_values.at[:, :halo_reach]
        .add(from_prev[1])
        .at[:, inner - halo_reach :]
        .add(from_next[1])
    )
    return (core_keys, core_values)


def fold_cols(acc_keys, acc_values, halo_reach):
    inner = acc_keys.shape[2] - 2 * halo_reach
    low_rims = jnp.stack([acc_keys[:, :, :halo_reach], acc_values[:, :, :halo_reach]])
    high_rims = jnp.stack(
        [acc_keys[:, :, inner + halo_reach :], acc_values[:, :, inner + halo_reach :]]
    )
    from_next = passed_along(low_rims.astype(jnp.bfloat16), "gy", -1).astype(low_rims.dtype)
    from_prev = passed_along(high_rims.astype(jnp.bfloat16), "gy", 1).astype(high_rims.dtype)
    core_keys = acc_keys[:, :, halo_reach : halo_reach + inner]
    core_keys = (
        core_keys.at[:, :, :halo_reach]
        .add(from_prev[0])
        .at[:, :, inner - halo_reach :]
        .add(from_next[0])
    )
    core_values = acc_values[:, :, halo_reach : halo_reach + inner]
    core_values = (
        core_values.at[:, :, :halo_reach]
        .add(from_prev[1])
        .at[:, :, inner - halo_reach :]
        .add(from_next[1])
    )
    return (core_keys, core_values)


def per_device(saved_queries, saved_keys, saved_values, out_grad, shifts):
    rows_x, cols_y, depth_len, channels = saved_queries.shape
    frame_count = saved_keys.shape[0]
    halo_reach = 2 + SMAX
    score_scale = 1.0 / math.sqrt(HD)
    span_y = BLOCK_Y
    span_z = BLOCK_Z
    total_x = rows_x * lax.axis_size("gx")
    total_y = cols_y * lax.axis_size("gy")
    first_x = lax.axis_index("gx") * rows_x
    first_y = lax.axis_index("gy") * cols_y
    pair_kv = jnp.stack([saved_keys, saved_values])
    halo_pair = with_halo(pair_kv, (("gx", 2), ("gy", 3)), halo_reach)
    halo_pair = jnp.pad(halo_pair, ((0, 0), (0, 0), (0, 0), (0, 0), (1, 1), (0, 0)))
    offsets = jnp.concatenate([jnp.zeros((1, 2), jnp.int32), shifts], 0)
    region_shape = (rows_x + 4, span_y + 4, span_z + 2)
    region_rows = region_shape[0] * region_shape[1] * region_shape[2]
    window = window_table(rows_x, span_y, span_z)
    blocks_z = depth_len // span_z
    block_total = cols_y // span_y * blocks_z
    relative_shape = (2, frame_count, rows_x + 4, cols_y + 4, depth_len + 2, channels)

    def one_block(block_id, state_tuple):
        grad_q, acc_pair, stat_field = state_tuple
        y_start = block_id // blocks_z * span_y
        z_start = block_id % blocks_z * span_z
        query_rows = lax.dynamic_slice(
            saved_queries, (0, y_start, z_start, 0), (rows_x, span_y, span_z, channels)
        )
        query_rows = query_rows.reshape(-1, HEADS, HD)
        grad_rows = lax.dynamic_slice(
            out_grad, (0, y_start, z_start, 0), (rows_x, span_y, span_z, channels)
        )
        grad_rows = grad_rows.reshape(-1, HEADS, HD)
        region_parts = []
        mask_parts = []
        for frame_id in range(frame_count):
            shift_x = offsets[frame_id, 0]
            shift_y = offsets[frame_id, 1]
            corner = (
                frame_id,
                halo_reach + shift_x - 2,
                halo_reach + shift_y - 2 + y_start,
                z_start,
                0,
            )
            piece = lax.dynamic_slice(halo_pair, (0,) + corner, (2, 1) + region_shape + (channels,))
            region_parts.append(piece.reshape(2, region_rows, HEADS, HD))
            grid_x = first_x + jnp.arange(region_shape[0], dtype=jnp.int32) + shift_x - 2
            grid_y = first_y + y_start + jnp.arange(region_shape[1], dtype=jnp.int32) + shift_y - 2
            grid_z = z_start + jnp.arange(region_shape[2], dtype=jnp.int32) - 1
            inside_x = (grid_x >= 0) & (grid_x < total_x)
            inside_y = (grid_y >= 0) & (grid_y < total_y)
            inside_z = (grid_z >= 0) & (grid_z < depth_len)
            in_grid = (
                inside_x[:, None, None] & inside_y[None, :, None] & inside_z[None, None, :]
            ).reshape(-1)
            mask_parts.append(window & in_grid[None, :])
        region_all = jnp.concatenate(region_parts, 1)
        key_rows = region_all[0]
        value_rows = region_all[1]
        mask_all = jnp.concatenate(mask_parts, 1)[None]
        scores = (
            jnp.einsum("qhd,khd->hqk", query_rows, key_rows, preferred_element_type=jnp.float32)
            * score_scale
        )
        scores = jnp.where(mask_all, scores, -1e30)
        row_max = jnp.max(scores, -1, keepdims=True)
        exp_scores = jnp.where(mask_all, jnp.exp(scores - row_max), 0.0)
        row_total = jnp.sum(exp_scores, -1, keepdims=True)
        attention = exp_scores / row_total
        grad_att = jnp.einsum(
            "qhd,khd->hqk", grad_rows, value_rows, preferred_element_type=jnp.float32
        )
        row_delta = jnp.sum(attention * grad_att, -1, keepdims=True)
        grad_scores = (attention * (grad_att - row_delta)).astype(jnp.bfloat16)
        block_dq = (
            jnp.einsum("hqk,khd->qhd", grad_scores, key_rows, preferred_element_type=jnp.float32)
            * score_scale
        )
        block_dq = block_dq.astype(jnp.bfloat16).reshape(rows_x, span_y, span_z, channels)
        grad_q = lax.dynamic_update_slice(grad_q, block_dq, (0, y_start, z_start, 0))
        weights = attention.astype(jnp.bfloat16)
        key_terms = (
            jnp.einsum("hqk,qhd->khd", grad_scores, query_rows, preferred_element_type=jnp.float32)
            * score_scale
        )
        value_terms = jnp.einsum(
            "hqk,qhd->khd", weights, grad_rows, preferred_element_type=jnp.float32
        )
        both_terms = jnp.stack([key_terms, value_terms]).reshape(
            (2, frame_count) + region_shape + (channels,)
        )
        place = (0, 0, 0, y_start, z_start, 0)
        size_tuple = (2, frame_count) + region_shape + (channels,)
        old_terms = lax.dynamic_slice(acc_pair, place, size_tuple)
        acc_pair = lax.dynamic_update_slice(acc_pair, old_terms + both_terms, place)
        return (grad_q, acc_pair, stat_field)

    acc_start = jnp.zeros(relative_shape, jnp.float32)
    stat_start = jnp.zeros((1,), jnp.float32)
    start_state = (
        jnp.zeros((rows_x, cols_y, depth_len, channels), jnp.bfloat16),
        acc_start,
        stat_start,
    )
    grad_q, acc_pair, stat_field = lax.fori_loop(0, block_total, one_block, start_state)
    placed_shape = (2, rows_x + 2 * halo_reach, cols_y + 2 * halo_reach, depth_len + 2, channels)
    placed_frames = []
    for frame_id in range(frame_count):
        start_x = halo_reach - 2 + offsets[frame_id, 0]
        start_y = halo_reach - 2 + offsets[frame_id, 1]
        placed = lax.dynamic_update_slice(
            jnp.zeros(placed_shape, jnp.float32), acc_pair[:, frame_id], (0, start_x, start_y, 0, 0)
        )
        placed_frames.append(placed)
    placed_all = jnp.stack(placed_frames, 1)
    acc_keys = placed_all[0, :, :, :, 1:-1]
    acc_values = placed_all[1, :, :, :, 1:-1]
    acc_keys, acc_values = fold_rows(acc_keys, acc_values, halo_reach)
    acc_keys, acc_values = fold_cols(acc_keys, acc_values, halo_reach)
    return (grad_q, acc_keys.astype(jnp.bfloat16), acc_values.astype(jnp.bfloat16))


def solution(mesh):
    placed = (
        P("gx", "gy", None, None),
        P(None, "gx", "gy", None, None),
        P(None, "gx", "gy", None, None),
        P("gx", "gy", None, None),
        P(),
    )
    return jax.shard_map(
        per_device,
        mesh=mesh,
        in_specs=placed,
        out_specs=(
            P("gx", "gy", None, None),
            P(None, "gx", "gy", None, None),
            P(None, "gx", "gy", None, None),
        ),
        check_vma=False,
    )
```

profile of v0, /device:TPU:40, one launch (start us, length us, event | category | flops | bytes accessed | tf_op | source)
XLA Modules:
  0.0 570.5 jit_solution(13425117377756573824)
XLA Ops:
  7.8 7.6 %collective-permute-done.1 = bf16[2,4,3,8,16,128]{5,4,3,2,1,0:T(8,128)(2,1)S(1)} collective-permute-done((bf16[2,4,3,8,16,128]{5,4,3,2,1,0:T(8,128)(2,1)S(1)}, bf16[2,4,3,8,16,128]{5,4,3,2,1,0:T(8,128)(2,1)S(1)}, u32[]{:S(2)}, u32[]{:S(2)}) %collective-permute-start.1) | collective-permute-done | bytes 786464 | tf_op jit(solution)/shard_map/ppermute | solution.py:30
  15.4 5.9 %collective-permute-done = bf16[2,4,3,8,16,128]{5,4,3,2,1,0:T(8,128)(2,1)S(1)} collective-permute-done((bf16[2,4,3,8,16,128]{5,4,3,2,1,0:T(8,128)(2,1)S(1)}, bf16[2,4,3,8,16,128]{5,4,3,2,1,0:T(8,128)(2,1)S(1)}, u32[]{:S(2)}, u32[]{:S(2)}) %collective-permute-start) | collective-permute-done | bytes 786464 | tf_op jit(solution)/shard_map/ppermute | solution.py:27
  24.1 9.0 %collective-permute-start.3 = (bf16[2,4,10,3,16,128]{5,4,3,2,1,0:T(8,128)(2,1)}, bf16[2,4,10,3,16,128]{5,4,3,2,1,0:T(8,128)(2,1)}, u32[]{:S(2)}, u32[]{:S(2)}) collective-permute-start(bf16[2,4,10,3,16,128]{5,4,3,2,1,0:T(8,128)(2,1)} %get-tuple-element.642), channel_id=1, source_target_pairs={{1,0},{2,1},{3,2},{4,3},{5,4},{6,5},{7,6},{9,8},{10,9},{11,10},{12... | collective-permute-start | bytes 2949128 | tf_op jit(solution)/shard_map/ppermute | solution.py:30
  43.4 39.1 %collective-permute-done.3 = bf16[2,4,10,3,16,128]{5,4,3,2,1,0:T(8,128)(2,1)} collective-permute-done((bf16[2,4,10,3,16,128]{5,4,3,2,1,0:T(8,128)(2,1)}, bf16[2,4,10,3,16,128]{5,4,3,2,1,0:T(8,128)(2,1)}, u32[]{:S(2)}, u32[]{:S(2)}) %collective-permute-start.3) | collective-permute-done | bytes 983072 | tf_op jit(solution)/shard_map/ppermute | solution.py:30
  82.5 30.6 %collective-permute-done.2 = bf16[2,4,10,3,16,128]{5,4,3,2,1,0:T(8,128)(2,1)} collective-permute-done((bf16[2,4,10,3,16,128]{5,4,3,2,1,0:T(8,128)(2,1)}, bf16[2,4,10,3,16,128]{5,4,3,2,1,0:T(8,128)(2,1)}, u32[]{:S(2)}, u32[]{:S(2)}) %collective-permute-start.2) | collective-permute-done | bytes 983072 | tf_op jit(solution)/shard_map/ppermute | solution.py:27
  116.8 11.5 %copy.43 = bf16[2,4,10,14,16,128]{5,0,4,3,2,1:T(2,128)(2,1)} copy(bf16[2,4,10,14,16,128]{5,4,3,2,1,0:T(8,128)(2,1)} %pad_maximum_fusion.3) | data formatting | bytes 9175040
  128.3 8.5 %pad.21.clone = bf16[2,4,10,14,18,128]{5,0,4,3,2,1:T(2,128)(2,1)} pad(bf16[2,4,10,14,16,128]{5,0,4,3,2,1:T(2,128)(2,1)} %copy.43, bf16[]{:T(256)} %constant.490.clone.1), padding=0_0x0_0x0_0x0_0x1_1x0_0 | pad | bytes 9748482 | tf_op jit(solution)/shard_map/jit(_pad)/pad | solution.py:109
  137.5 4.8 broadcast_in_dim.95
  142.3 351.3 %while.27 = (s32[]{:T(128)}, bf16[4,8,16,128]{3,2,1,0:T(8,128)(2,1)}, f32[2,4,8,12,18,128]{5,4,3,2,1,0:T(8,128)}, bf16[2,4,10,14,18,128]{5,0,4,3,2,1:T(2,128)(2,...) while((s32[]{:T(128)}, ...), condition=%wide.region_4.5_spmd.clone, body=%wide.region_0.4_spmd.sunk.clone.sunk | while | flops 395809632 | bytes 91650816 | solution.py:202
  163.9 5.3 fusion.63
  183.3 5.3 stack.109
  193.1 5.3 stack.110
  198.4 4.4 maximum_add_fusion.2
  202.9 27.3 %dynamic_update_slice.55 = f32[2,4,8,12,18,128]{5,4,3,2,1,0:T(8,128)} dynamic-update-slice(f32[2,4,8,12,18,128]{5,4,3,2,1,0:T(8,128)} %get-tuple-element.849, f32[2,4,8,12,6,128]{5,4,3,2,1,0:T(8,128)S(1)} %maximum_add_fusion.2, s32[]{:T(128)} %constant.489.clone.1..sunk, s32[]{:T(128)} %constant.489.clone.1..sunk, s32[]{:T(128)} %constant.489.clone.1..sunk, s32[]{:T(128)} %constant.489.clone.1..sunk, ...) | dynamic-update-slice | bytes 4718596 | tf_op jit(solution)/shard_map/while/body/eval_jaxpr/dynamic_update_slice | solution.py:192
  251.8 5.3 fusion.63
  271.1 5.3 stack.109
  281.0 5.3 stack.110
  286.3 4.4 maximum_add_fusion.2
  290.7 27.3 %dynamic_update_slice.55 = f32[2,4,8,12,18,128]{5,4,3,2,1,0:T(8,128)} dynamic-update-slice(f32[2,4,8,12,18,128]{5,4,3,2,1,0:T(8,128)} %get-tuple-element.849, f32[2,4,8,12,6,128]{5,4,3,2,1,0:T(8,128)S(1)} %maximum_add_fusion.2, s32[]{:T(128)} %constant.489.clone.1..sunk, s32[]{:T(128)} %constant.489.clone.1..sunk, s32[]{:T(128)} %constant.489.clone.1..sunk, s32[]{:T(128)} %constant.489.clone.1..sunk, ...) | dynamic-update-slice | bytes 4718596 | tf_op jit(solution)/shard_map/while/body/eval_jaxpr/dynamic_update_slice | solution.py:192
  339.6 5.3 fusion.63
  359.0 5.3 stack.109
  368.9 5.3 stack.110
  378.6 27.3 %dynamic_update_slice.55 = f32[2,4,8,12,18,128]{5,4,3,2,1,0:T(8,128)} dynamic-update-slice(f32[2,4,8,12,18,128]{5,4,3,2,1,0:T(8,128)} %get-tuple-element.849, f32[2,4,8,12,6,128]{5,4,3,2,1,0:T(8,128)S(1)} %maximum_add_fusion.2, s32[]{:T(128)} %constant.489.clone.1..sunk, s32[]{:T(128)} %constant.489.clone.1..sunk, s32[]{:T(128)} %constant.489.clone.1..sunk, s32[]{:T(128)} %constant.489.clone.1..sunk, ...) | dynamic-update-slice | bytes 4718596 | tf_op jit(solution)/shard_map/while/body/eval_jaxpr/dynamic_update_slice | solution.py:192
  427.4 5.3 fusion.63
  446.8 5.3 stack.109
  456.7 5.3 stack.110
  466.4 27.3 %dynamic_update_slice.55 = f32[2,4,8,12,18,128]{5,4,3,2,1,0:T(8,128)} dynamic-update-slice(f32[2,4,8,12,18,128]{5,4,3,2,1,0:T(8,128)} %get-tuple-element.849, f32[2,4,8,12,6,128]{5,4,3,2,1,0:T(8,128)S(1)} %maximum_add_fusion.2, s32[]{:T(128)} %constant.489.clone.1..sunk, s32[]{:T(128)} %constant.489.clone.1..sunk, s32[]{:T(128)} %constant.489.clone.1..sunk, s32[]{:T(128)} %constant.489.clone.1..sunk, ...) | dynamic-update-slice | bytes 4718596 | tf_op jit(solution)/shard_map/while/body/eval_jaxpr/dynamic_update_slice | solution.py:192
  504.0 5.8 %collective-permute-start.5 = (bf16[2,4,3,14,16,128]{5,4,3,2,1,0:T(8,128)(2,1)S(1)}, bf16[2,4,3,14,16,128]{5,4,3,2,1,0:T(8,128)(2,1)S(1)}, u32[]{:S(2)}, u32[]{:S(2)}) collective-permute-start(bf16[2,4,3,14,16,128]{5,4,3,2,1,0:T(8,128)(2,1)S(1)} %pad_maximum_fusion.5), channel_id=1, source_target_pairs={{8,0},{16,8},{24,16},{32,24},{40,32},{48,40},{56,48},{64,56},{72,6... | collective-permute-start | bytes 4128776 | tf_op jit(solution)/shard_map/ppermute | solution.py:19
  510.0 13.7 %collective-permute-done.4 = bf16[2,4,3,14,16,128]{5,4,3,2,1,0:T(8,128)(2,1)S(1)} collective-permute-done((bf16[2,4,3,14,16,128]{5,4,3,2,1,0:T(8,128)(2,1)S(1)}, bf16[2,4,3,14,16,128]{5,4,3,2,1,0:T(8,128)(2,1)S(1)}, u32[]{:S(2)}, u32[]{:S(2)}) %collective-permute-start.4) | collective-permute-done | bytes 1376288 | tf_op jit(solution)/shard_map/ppermute | solution.py:19
  526.9 8.3 %collective-permute-start.6 = (bf16[2,4,4,3,16,128]{5,4,3,2,1,0:T(8,128)(2,1)S(1)}, bf16[2,4,4,3,16,128]{5,4,3,2,1,0:T(8,128)(2,1)S(1)}, u32[]{:S(2)}, u32[]{:S(2)}) collective-permute-start(bf16[2,4,4,3,16,128]{5,4,3,2,1,0:T(8,128)(2,1)S(1)} %pad_maximum_fusion.11), channel_id=1, source_target_pairs={{0,1},{1,2},{2,3},{3,4},{4,5},{5,6},{6,7},{8,9},{9,10},{10,11},{11... | collective-permute-start | bytes 1179656 | tf_op jit(solution)/shard_map/ppermute | solution.py:19
  537.8 24.3 %collective-permute-done.6 = bf16[2,4,4,3,16,128]{5,4,3,2,1,0:T(8,128)(2,1)S(1)} collective-permute-done((bf16[2,4,4,3,16,128]{5,4,3,2,1,0:T(8,128)(2,1)S(1)}, bf16[2,4,4,3,16,128]{5,4,3,2,1,0:T(8,128)(2,1)S(1)}, u32[]{:S(2)}, u32[]{:S(2)}) %collective-permute-start.6) | collective-permute-done | bytes 393248 | tf_op jit(solution)/shard_map/ppermute | solution.py:19
  562.3 6.1 %collective-permute-done.7 = bf16[2,4,4,3,16,128]{5,4,3,2,1,0:T(8,128)(2,1)S(1)} collective-permute-done((bf16[2,4,4,3,16,128]{5,4,3,2,1,0:T(8,128)(2,1)S(1)}, bf16[2,4,4,3,16,128]{5,4,3,2,1,0:T(8,128)(2,1)S(1)}, u32[]{:S(2)}, u32[]{:S(2)}) %collective-permute-start.7) | collective-permute-done | bytes 393248 | tf_op jit(solution)/shard_map/ppermute | solution.py:19
  (245 shorter events, 204.7 us)
Async XLA Ops:
  0.6 34.5 %copy-start.6 = (s32[3,2]{0,1:T(2,128)S(1)}, s32[3,2]{0,1:T(2,128)}, u32[]{:S(2)}) copy-start(s32[3,2]{0,1:T(2,128)} %param.28) | copy-start | bytes 76
  0.6 112.5 %copy-start.2 = (bf16[4,4,8,16,128]{4,3,2,1,0:T(8,128)(2,1)S(1)}, bf16[4,4,8,16,128]{4,3,2,1,0:T(8,128)(2,1)}, u32[]{:S(2)}) copy-start(bf16[4,4,8,16,128]{4,3,2,1,0:T(8,128)(2,1)} %param.25) | copy-start | bytes 1572868
  0.7 112.5 %copy-start.3 = (bf16[4,4,8,16,128]{4,3,2,1,0:T(8,128)(2,1)S(1)}, bf16[4,4,8,16,128]{4,3,2,1,0:T(8,128)(2,1)}, u32[]{:S(2)}) copy-start(bf16[4,4,8,16,128]{4,3,2,1,0:T(8,128)(2,1)} %param.26) | copy-start | bytes 1572868
  2.2 13.1 %collective-permute-start.1 = (bf16[2,4,3,8,16,128]{5,4,3,2,1,0:T(8,128)(2,1)S(1)}, bf16[2,4,3,8,16,128]{5,4,3,2,1,0:T(8,128)(2,1)S(1)}, u32[]{:S(2)}, u32[]{:S(2)}) collective-permute-start(bf16[2,4,3,8,16,128]{5,4,3,2,1,0:T(8,128)(2,1)S(1)} %get-tuple-element.648), channel_id=1, source_target_pairs={{8,0},{16,8},{24,16},{32,24},{40,32},{48,40},{56,48},{64,56},{72,6... | collective-permute-start | bytes 2359304 | tf_op jit(solution)/shard_map/ppermute | solution.py:30
  5.9 15.4 %collective-permute-start = (bf16[2,4,3,8,16,128]{5,4,3,2,1,0:T(8,128)(2,1)S(1)}, bf16[2,4,3,8,16,128]{5,4,3,2,1,0:T(8,128)(2,1)S(1)}, u32[]{:S(2)}, u32[]{:S(2)}) collective-permute-start(bf16[2,4,3,8,16,128]{5,4,3,2,1,0:T(8,128)(2,1)S(1)} %get-tuple-element.647), channel_id=1, source_target_pairs={{0,8},{8,16},{16,24},{24,32},{32,40},{40,48},{48,56},{56,64},{64,7... | collective-permute-start | bytes 2359304 | tf_op jit(solution)/shard_map/ppermute | solution.py:27
  24.1 58.5 %collective-permute-start.3 = (bf16[2,4,10,3,16,128]{5,4,3,2,1,0:T(8,128)(2,1)}, bf16[2,4,10,3,16,128]{5,4,3,2,1,0:T(8,128)(2,1)}, u32[]{:S(2)}, u32[]{:S(2)}) collective-permute-start(bf16[2,4,10,3,16,128]{5,4,3,2,1,0:T(8,128)(2,1)} %get-tuple-element.642), channel_id=1, source_target_pairs={{1,0},{2,1},{3,2},{4,3},{5,4},{6,5},{7,6},{9,8},{10,9},{11,10},{12... | collective-permute-start | bytes 2949128 | tf_op jit(solution)/shard_map/ppermute | solution.py:30
  33.0 80.1 %collective-permute-start.2 = (bf16[2,4,10,3,16,128]{5,4,3,2,1,0:T(8,128)(2,1)}, bf16[2,4,10,3,16,128]{5,4,3,2,1,0:T(8,128)(2,1)}, u32[]{:S(2)}, u32[]{:S(2)}) collective-permute-start(bf16[2,4,10,3,16,128]{5,4,3,2,1,0:T(8,128)(2,1)} %get-tuple-element.641), channel_id=1, source_target_pairs={{0,1},{1,2},{2,3},{3,4},{4,5},{5,6},{6,7},{8,9},{9,10},{10,11},{11... | collective-permute-start | bytes 2949128 | tf_op jit(solution)/shard_map/ppermute | solution.py:27
  163.9 5.3 copy-start.4
  169.4 3.4 copy-start.5
  169.4 3.8 copy-start.1
  251.8 5.3 copy-start.4
  257.3 3.4 copy-start.5
  257.3 3.8 copy-start.1
  339.6 5.3 copy-start.4
  345.1 3.4 copy-start.5
  345.1 3.8 copy-start.1
  427.4 5.3 copy-start.4
  432.9 3.4 copy-start.5
  432.9 3.8 copy-start.1
  493.7 4.4 copy-start
  501.9 21.7 %collective-permute-start.4 = (bf16[2,4,3,14,16,128]{5,4,3,2,1,0:T(8,128)(2,1)S(1)}, bf16[2,4,3,14,16,128]{5,4,3,2,1,0:T(8,128)(2,1)S(1)}, u32[]{:S(2)}, u32[]{:S(2)}) collective-permute-start(bf16[2,4,3,14,16,128]{5,4,3,2,1,0:T(8,128)(2,1)S(1)} %pad_maximum_fusion.4), channel_id=1, source_target_pairs={{0,8},{8,16},{16,24},{24,32},{32,40},{40,48},{48,56},{56,64},{64,7... | collective-permute-start | bytes 4128776 | tf_op jit(solution)/shard_map/ppermute | solution.py:19
  504.0 21.6 %collective-permute-start.5 = (bf16[2,4,3,14,16,128]{5,4,3,2,1,0:T(8,128)(2,1)S(1)}, bf16[2,4,3,14,16,128]{5,4,3,2,1,0:T(8,128)(2,1)S(1)}, u32[]{:S(2)}, u32[]{:S(2)}) collective-permute-start(bf16[2,4,3,14,16,128]{5,4,3,2,1,0:T(8,128)(2,1)S(1)} %pad_maximum_fusion.5), channel_id=1, source_target_pairs={{8,0},{16,8},{24,16},{32,24},{40,32},{48,40},{56,48},{64,56},{72,6... | collective-permute-start | bytes 4128776 | tf_op jit(solution)/shard_map/ppermute | solution.py:19
  526.9 35.3 %collective-permute-start.6 = (bf16[2,4,4,3,16,128]{5,4,3,2,1,0:T(8,128)(2,1)S(1)}, bf16[2,4,4,3,16,128]{5,4,3,2,1,0:T(8,128)(2,1)S(1)}, u32[]{:S(2)}, u32[]{:S(2)}) collective-permute-start(bf16[2,4,4,3,16,128]{5,4,3,2,1,0:T(8,128)(2,1)S(1)} %pad_maximum_fusion.11), channel_id=1, source_target_pairs={{0,1},{1,2},{2,3},{3,4},{4,5},{5,6},{6,7},{8,9},{9,10},{10,11},{11... | collective-permute-start | bytes 1179656 | tf_op jit(solution)/shard_map/ppermute | solution.py:19
  535.3 33.2 %collective-permute-start.7 = (bf16[2,4,4,3,16,128]{5,4,3,2,1,0:T(8,128)(2,1)S(1)}, bf16[2,4,4,3,16,128]{5,4,3,2,1,0:T(8,128)(2,1)S(1)}, u32[]{:S(2)}, u32[]{:S(2)}) collective-permute-start(bf16[2,4,4,3,16,128]{5,4,3,2,1,0:T(8,128)(2,1)S(1)} %pad_maximum_fusion.12), channel_id=1, source_target_pairs={{1,0},{2,1},{3,2},{4,3},{5,4},{6,5},{7,6},{9,8},{10,9},{11,10},{12... | collective-permute-start | bytes 1179656 | tf_op jit(solution)/shard_map/ppermute | solution.py:19
where the time goes:
time: 578 us; the launch traced here: 570 us
  local copies, waits for them, and re-layouts  285 us (49%)
  waiting for transfers between devices  128 us (22%)
  matrix products  56.9 us (10%)
  other arithmetic  55.7 us (10%)
  starting transfers between devices  34.9 us (6%)
  between operations  8.62 us (1%)
    dynamic_update_slice x4, local copies, waits for them, and re-layouts, one_block(): acc_pair = lax.dynamic_update_slice(acc_pair, old_terms + both_terms, place)  109 us
    ppermute x2, waiting for transfers between devices, with_halo(): lax.ppermute(lax.slice_in_dim(block, 0, width, axis=dim), axis, backward)  46.7 us
    ppermute x4, waiting for transfers between devices, passed_along(): return lax.ppermute(shard, axis, pairs)  45.3 us
    another operation x8, local copies, waits for them, and re-layouts, one_block(): jnp.stack([key_terms, value_terms])  42.1 us
    ppermute x2, waiting for transfers between devices, with_halo(): lax.ppermute(lax.slice_in_dim(block, block.shape[dim] - width, None, axis...  36.5 us
    reshape x32, local copies, waits for them, and re-layouts, one_block(): region_parts.append(piece.reshape(2, region_rows, HEADS, HD))  27.1 us
    sub x4, matrix products, one_block(): exp_scores = jnp.where(mask_all, jnp.exp(scores - row_max), 0.0)  21.1 us
    ppermute x4, starting transfers between devices, passed_along(): return lax.ppermute(shard, axis, pairs)  18.3 us
  transfers between devices with their start and end apart: 8, of which 8 were waited for; matrix products, arithmetic and copies ran while one was open for 0% of the time, Pallas kernels for 0%

commit v1 on v0

v1 whole, which is shorter than its diff:
```python
import functools
import math

import jax
import jax.numpy as jnp
import numpy as np
from jax import lax
from jax.experimental import pallas as pl
from jax.experimental.pallas import tpu as pltpu
from jax.sharding import PartitionSpec as P

HEADS = 4
HD = 32
C = 128
Z = 16
FRAMES = 4
R = 3
BX = 4
BY = 8
HX = BX + 2 * R
HY = BY + 2 * R
SCALE = 1.0 / math.sqrt(HD)
C2 = SCALE * math.log2(math.e)
NEG = -1e30
KEYS_Y = ((0, 2), (0, 4), (0, 6), (2, 8), (4, 8), (6, 8))


def bias_table():
    rx = np.arange(6) - 2
    col = np.arange(4)
    cx, cy = col // 2, col % 2
    okx = np.abs(rx[:, None] - cx[None]) <= 2
    oky = np.abs(rx[:, None] - cy[None]) <= 2
    z = np.arange(Z)
    okz = np.abs(z[:, None] - z[None]) <= 1
    ok = okx[:, None, None, :, None, None] & oky[None, :, None, :, None, None]
    ok = ok & okz[None, None, :, None, None, :]
    ok = np.broadcast_to(ok, (6, 6, Z, 4, HEADS, Z)).reshape(6, 6, Z, 4 * HEADS * Z)
    return jnp.asarray(np.where(ok, 0.0, NEG).astype(np.float32))


def head_masks():
    lane = lax.broadcasted_iota(jnp.int32, (Z, C), 1) // HD
    return [jnp.where(lane == h, 1.0, 0.0).astype(jnp.bfloat16) for h in range(HEADS)]


def expanded(ref, x, y, masks):
    parts = []
    for cx in range(2):
        for cy in range(2):
            column = ref[x + cx, y + cy]
            parts += [column * mask for mask in masks]
    return jnp.concatenate(parts, 0)


def dot_t(a, b):
    return lax.dot_general(a, b, (((1,), (1,)), ((), ())), preferred_element_type=jnp.float32)


def dot_n(a, b):
    return lax.dot_general(a, b, (((1,), (0,)), ((), ())), preferred_element_type=jnp.float32)


def dot_l(a, b):
    return lax.dot_general(a, b, (((0,), (0,)), ((), ())), preferred_element_type=jnp.float32)


def low_half():
    return lax.broadcasted_iota(jnp.int32, (1, C), 1) < C // 2


def blocks(body, f):
    def step(j, carry):
        for by in range(6):
            body(3 * j, 2, 2 * j, by)
        for by in range(6):
            body(1 + j, 4, 0, by)
        return carry

    lax.fori_loop(0, 2, step, 0)


def window_start(shifts_ref, f):
    past = jnp.maximum(f - 1, 0)
    ox = jnp.where(f > 0, shifts_ref[past, 0], 0)
    oy = jnp.where(f > 0, shifts_ref[past, 1], 0)
    return 1 - ox, 1 - oy


def stats_kernel(shifts_ref, q_ref, g_ref, k_ref, v_ref, bias_ref, out_ref, lse_w, dn_w):
    masks = head_masks()
    low = low_half()
    lse_w[...] = jnp.full(lse_w.shape, NEG, jnp.float32)
    dn_w[...] = jnp.zeros(dn_w.shape, jnp.float32)

    def frame(f, carry):
        sx, sy = window_start(shifts_ref, f)

        def body(bx, nx, kx0, by):
            y0, y1 = KEYS_Y[by]
            rows = nx * (y1 - y0) * Z
            qe = expanded(q_ref, sx + 2 * bx, sy + 2 * by, masks)
            ge = expanded(g_ref, sx + 2 * bx, sy + 2 * by, masks)
            kt = k_ref[f, pl.ds(kx0, nx), y0:y1].reshape(rows, C)
            vt = v_ref[f, pl.ds(kx0, nx), y0:y1].reshape(rows, C)
            r0 = y0 + 4 - 2 * by
            bias = bias_ref[pl.ds(kx0 + 4 - 2 * bx, nx), r0 : r0 + y1 - y0].reshape(rows, 256)
            t = (dot_t(kt, qe) + bias).reshape(rows // 8, 8, 256)
            ga = dot_t(vt, ge).reshape(rows // 8, 8, 256)
            m = jnp.max(t, 0)
            e = jnp.exp2((t - m[None]) * C2)
            l = jnp.sum(e, 0)
            d = jnp.sum(e * ga, 0)
            top = jnp.max(m, 0, keepdims=True)
            w = jnp.exp2((m - top) * C2)
            l = jnp.sum(l * w, 0, keepdims=True)
            d = jnp.sum(d * w, 0, keepdims=True)
            lse = top * C2 + jnp.log2(l)
            dn = d / l
            for cx in range(2):
                for val, dst in ((lse, lse_w), (dn, dn_w)):
                    v2 = val[:, cx * C : (cx + 1) * C]
                    other = pltpu.roll(v2, C // 2, 1)
                    dst[f, 2 + 2 * bx + cx, 2 + 2 * by : 3 + 2 * by] = jnp.where(low, v2, other)
                    dst[f, 2 + 2 * bx + cx, 3 + 2 * by : 4 + 2 * by] = jnp.where(low, other, v2)

        blocks(body, f)
        return carry

    lax.fori_loop(0, FRAMES, frame, 0)

    def merge(r, carry):
        ls, ds = [], []
        for f in range(FRAMES):
            sx, sy = window_start(shifts_ref, f)
            ls.append(lse_w[f, r + 2 - sx, pl.ds(2 - sy, 16)])
            ds.append(dn_w[f, r + 2 - sx, pl.ds(2 - sy, 16)])
        top = functools.reduce(jnp.maximum, ls)
        ws = [jnp.exp2(x - top) for x in ls]
        total = sum(ws)
        mean = sum(w * x for w, x in zip(ws, ds)) / total
        out_ref[r] = jnp.where(low, top + jnp.log2(total), mean)
        return carry

    lax.fori_loop(0, HX, merge, 0)


def grads_kernel(
    shifts_ref, q_ref, g_ref, k_ref, v_ref, st_ref, bias_ref, dq_ref, dk_ref, dv_ref, dk_a, dv_a, dq_w
):
    masks = head_masks()
    low = low_half()
    head_of_lane = lax.broadcasted_iota(jnp.int32, (Z, C), 1) // HD
    dq_w[...] = jnp.zeros(dq_w.shape, jnp.float32)

    def frame(f, carry):
        sx, sy = window_start(shifts_ref, f)
        dk_a[...] = jnp.zeros(dk_a.shape, jnp.float32)
        dv_a[...] = jnp.zeros(dv_a.shape, jnp.float32)

        def body(bx, nx, kx0, by):
            y0, y1 = KEYS_Y[by]
            ny = y1 - y0
            rows = nx * ny * Z
            xq, yq = sx + 2 * bx, sy + 2 * by
            qe = expanded(q_ref, xq, yq, masks)
            ge = expanded(g_ref, xq, yq, masks)
            lses, dels = [], []
            for cx in range(2):
                a = st_ref[xq + cx, pl.ds(yq, 1)]
                b = st_ref[xq + cx, pl.ds(yq + 1, 1)]
                lses.append(jnp.where(low, a, pltpu.roll(b, C // 2, 1)))
                dels.append(jnp.where(low, pltpu.roll(a, C // 2, 1), b))
            lse = jnp.concatenate(lses, 1)
            delta = jnp.concatenate(dels, 1)
            kt = k_ref[f, pl.ds(kx0, nx), y0:y1].reshape(rows, C)
            vt = v_ref[f, pl.ds(kx0, nx), y0:y1].reshape(rows, C)
            r0 = y0 + 4 - 2 * by
            bias = bias_ref[pl.ds(kx0 + 4 - 2 * bx, nx), r0 : r0 + ny].reshape(rows, 256)
            att = jnp.exp2((dot_t(kt, qe) + bias) * C2 - lse)
            gs = (att * (dot_t(vt, ge) - delta)).astype(jnp.bfloat16)
            wt = att.astype(jnp.bfloat16)
            dk_a[pl.ds(kx0, nx), y0:y1] += dot_n(gs, qe).reshape(nx, ny, Z, C)
            dv_a[pl.ds(kx0, nx), y0:y1] += dot_n(wt, ge).reshape(nx, ny, Z, C)
            dq = dot_l(gs, kt)
            for cx in range(2):
                for cy in range(2):
                    base = (2 * cx + cy) * HEADS * Z
                    out = dq[base : base + Z]
                    for h in range(1, HEADS):
                        part = dq[base + h * Z : base + (h + 1) * Z]
                        out = jnp.where(head_of_lane == h, part, out)
                    dq_w[f, 2 + 2 * bx + cx, 2 + 2 * by + cy] = out

        blocks(body, f)
        dk_ref[f] = (dk_a[...] * SCALE).astype(jnp.bfloat16)
        dv_ref[f] = dv_a[...].astype(jnp.bfloat16)
        return carry

    lax.fori_loop(0, FRAMES, frame, 0)

    def merge(r, carry):
        total = jnp.zeros((HY, Z, C), jnp.float32)
        for f in range(FRAMES):
            sx, sy = window_start(shifts_ref, f)
            total = total + dq_w[f, r + 2 - sx, pl.ds(2 - sy, HY)]
        dq_ref[r] = total * SCALE
        return carry

    lax.fori_loop(0, HX, merge, 0)


def shifted(block, axis, by):
    n = lax.axis_size(axis)
    pairs = [(i, i + by) for i in range(n) if 0 <= i + by < n]
    return lax.ppermute(block, axis, pairs)


def with_halo(block, axis, dim):
    size = block.shape[dim]
    low = shifted(lax.slice_in_dim(block, size - R, size, axis=dim), axis, 1)
    high = shifted(lax.slice_in_dim(block, 0, R, axis=dim), axis, -1)
    return jnp.concatenate([low, block, high], dim)


def merged_stats(a, b):
    la, lb = a[..., : C // 2], b[..., : C // 2]
    top = jnp.maximum(la, lb)
    wa, wb = jnp.exp2(la - top), jnp.exp2(lb - top)
    total = wa + wb
    mean = (wa * a[..., C // 2 :] + wb * b[..., C // 2 :]) / total
    return jnp.concatenate([top + jnp.log2(total), mean], -1)


def added(block, axis, dim):
    size = block.shape[dim] - 2 * R
    cut = functools.partial(lax.slice_in_dim, block, axis=dim)
    from_next = shifted(cut(0, R).astype(jnp.bfloat16), axis, -1).astype(jnp.float32)
    from_prev = shifted(cut(size + R, size + 2 * R).astype(jnp.bfloat16), axis, 1).astype(jnp.float32)
    own = cut(R, R + size)
    pad_lo, pad_hi = [(0, 0, 0)] * own.ndim, [(0, 0, 0)] * own.ndim
    pad_lo[dim] = (0, size - R, 0)
    pad_hi[dim] = (size - R, 0, 0)
    zero = jnp.float32(0)
    return own + lax.pad(from_prev, zero, pad_lo) + lax.pad(from_next, zero, pad_hi)


def vmem(n):
    return [pl.BlockSpec(memory_space=pltpu.VMEM)] * n


def per_device(saved_queries, saved_keys, saved_values, out_grad, shifts):
    bias = bias_table()
    qg = jnp.stack([saved_queries, out_grad])
    qg = with_halo(with_halo(qg, "gy", 2), "gx", 1)
    q, g = qg[0], qg[1]
    params = pltpu.CompilerParams(vmem_limit_bytes=56 * 2**20)
    smem = [pl.BlockSpec(memory_space=pltpu.SMEM)]
    stats = pl.pallas_call(
        stats_kernel,
        out_shape=jax.ShapeDtypeStruct((HX, 16, C), jnp.float32),
        in_specs=smem + vmem(5),
        out_specs=pl.BlockSpec(memory_space=pltpu.VMEM),
        scratch_shapes=[pltpu.VMEM((FRAMES, 12, 24, C), jnp.float32)] * 2,
        compiler_params=params,
    )(shifts, q, g, saved_keys, saved_values, bias)
    stats = stats[:, :HY]
    absent = jnp.concatenate(
        [jnp.full((C // 2,), NEG, jnp.float32), jnp.zeros((C // 2,), jnp.float32)]
    )
    stats = fold_stats(fold_stats(stats, "gx", 0, absent), "gy", 1, absent)
    stats = with_halo(with_halo(stats, "gy", 1), "gx", 0)
    stats = jnp.pad(stats, ((0, 0), (0, 2), (0, 0)))
    block = jax.ShapeDtypeStruct(saved_keys.shape, jnp.bfloat16)
    dq, dk, dv = pl.pallas_call(
        grads_kernel,
        out_shape=(jax.ShapeDtypeStruct((HX, HY, Z, C), jnp.float32), block, block),
        in_specs=smem + vmem(6),
        out_specs=tuple(vmem(3)),
        scratch_shapes=[
            pltpu.VMEM((BX, BY, Z, C), jnp.float32),
            pltpu.VMEM((BX, BY, Z, C), jnp.float32),
            pltpu.VMEM((FRAMES, 12, 16, Z, C), jnp.float32),
        ],
        compiler_params=params,
    )(shifts, q, g, saved_keys, saved_values, stats, bias)
    dq = added(added(dq, "gx", 0), "gy", 1)
    return dq.astype(jnp.bfloat16), dk, dv


def fold_stats(block, axis, dim, absent):
    size = block.shape[dim] - 2 * R
    me, n = lax.axis_index(axis), lax.axis_size(axis)
    cut = functools.partial(lax.slice_in_dim, block, axis=dim)
    from_next = jnp.where(me < n - 1, shifted(cut(0, R), axis, -1), absent)
    from_prev = jnp.where(me > 0, shifted(cut(size + R, size + 2 * R), axis, 1), absent)
    own = cut(R, R + size)
    shape = list(own.shape)
    shape[dim] = size - R
    rest = jnp.broadcast_to(absent, shape)
    own = merged_stats(own, jnp.concatenate([from_prev, rest], dim))
    return merged_stats(own, jnp.concatenate([rest, from_next], dim))


def solution(mesh):
    block = P("gx", "gy", None, None)
    frames = P(None, "gx", "gy", None, None)
    return jax.shard_map(
        per_device,
        mesh=mesh,
        in_specs=(block, frames, frames, block, P()),
        out_specs=(block, frames, frames),
        check_vma=False,
    )
```

time: 578 us -> 162 us (0.28); the launches traced: 570 us -> 161 us
  local copies, waits for them, and re-layouts: 285 us -> 2.81 us
  waiting for transfers between devices: 128 us -> 33.4 us
  matrix products: 56.9 us -> 0 us
  other arithmetic: 55.7 us -> 7.19 us
  Pallas kernels: 0 us -> 42.9 us
  starting transfers between devices: 34.9 us -> 73.6 us
  between operations: 8.62 us -> 0.91 us
    dynamic_update_slice x11 -> x0, local copies, waits for them, and re-layouts: 112 us -> none  [the longest x4 109 us: one_block(): acc_pair = lax.dynamic_update_slice(acc_pair, old_terms + both_terms, place)]
    ppermute x8 -> x16, waiting for transfers between devices: 128 us -> 33.4 us  [shifted(): return lax.ppermute(block, axis, pairs)]
    another operation x15 -> x0, local copies, waits for them, and re-layouts: 43.6 us -> none  [the longest x8 42.1 us: one_block(): jnp.stack([key_terms, value_terms])]
    pallas_call x0 -> x2, Pallas kernels: none -> 42.9 us  [the longest x1 30.5 us: per_device(): pl.pallas_call(grads_kernel, out_shape=(jax.ShapeDtypeStruct((HX, HY, Z,...]
    ppermute x8 -> x16, starting transfers between devices: 34.9 us -> 73.6 us  [shifted(): return lax.ppermute(block, axis, pairs)]
    dot_general x16 -> x0, matrix products: 35.8 us -> none  [the longest x4 13.6 us: one_block(): jnp.einsum('qhd,khd->hqk', grad_rows, value_rows, preferred_element_type=...]
    reshape x52 -> x0, local copies, waits for them, and re-layouts: 31.7 us -> none  [the longest x32 27.1 us: one_block(): region_parts.append(piece.reshape(2, region_rows, HEADS, HD))]
    sub x4 -> x0, matrix products: 21.1 us -> none  [one_block(): exp_scores = jnp.where(mask_all, jnp.exp(scores - row_max), 0.0)]
  transfers between devices with their start and end apart: 8 -> 16, of which waited for: 8 -> 12; matrix products, arithmetic and copies ran while one was open for 0% -> 0% of each run, Pallas kernels for 0% -> 0%
where the time goes in v1:
time: 162 us; the launch traced here: 161 us
  starting transfers between devices  73.6 us (45%)
  Pallas kernels  42.9 us (26%)
  waiting for transfers between devices  33.4 us (21%)
  other arithmetic  7.19 us (4%)
  local copies, waits for them, and re-layouts  2.81 us (2%)
    ppermute x16, starting transfers between devices, shifted(): return lax.ppermute(block, axis, pairs)  73.6 us
    ppermute x16, waiting for transfers between devices, shifted(): return lax.ppermute(block, axis, pairs)  33.4 us
    pallas_call x1, Pallas kernels, per_device(): pl.pallas_call(grads_kernel, out_shape=(jax.ShapeDtypeStruct((HX, HY, Z,...  30.5 us
    pallas_call x1, Pallas kernels, per_device(): pl.pallas_call(stats_kernel, out_shape=jax.ShapeDtypeStruct((HX, 16, C),...  12.4 us
  transfers between devices with their start and end apart: 16, of which 12 were waited for; matrix products, arithmetic and copies ran while one was open for 0% of the time, Pallas kernels for 0%

profile of v1, /device:TPU:40, one launch (start us, length us, event | category | flops | bytes accessed | tf_op | source)
XLA Modules:
  0.0 160.8 jit_solution(10173076880972002259)
XLA Ops:
  1.5 8.2 %collective-permute-start = (bf16[2,4,3,16,128]{4,3,2,1,0:T(8,128)(2,1)S(1)}, bf16[2,4,3,16,128]{4,3,2,1,0:T(8,128)(2,1)S(1)}, u32[]{:S(2)}, u32[]{:S(2)}) collective-permute-start(bf16[2,4,3,16,128]{4,3,2,1,0:T(8,128)(2,1)S(1)} %get-tuple-element.17), channel_id=1, source_target_pairs={{0,1},{1,2},{2,3},{3,4},{4,5},{5,6},{6,7},{8,9},{9,10},{10,11},{11... | collective-permute-start | bytes 294920 | tf_op jit(solution)/shard_map/ppermute | solution.py:216
  9.8 2.6 %collective-permute-start.1 = (bf16[2,4,3,16,128]{4,3,2,1,0:T(8,128)(2,1)S(1)}, bf16[2,4,3,16,128]{4,3,2,1,0:T(8,128)(2,1)S(1)}, u32[]{:S(2)}, u32[]{:S(2)}) collective-permute-start(bf16[2,4,3,16,128]{4,3,2,1,0:T(8,128)(2,1)S(1)} %get-tuple-element.18), channel_id=1, source_target_pairs={{1,0},{2,1},{3,2},{4,3},{5,4},{6,5},{7,6},{9,8},{10,9},{11,10},{12... | collective-permute-start | bytes 294920 | tf_op jit(solution)/shard_map/ppermute | solution.py:216
  12.9 9.2 %collective-permute-done.1 = bf16[2,4,3,16,128]{4,3,2,1,0:T(8,128)(2,1)S(1)} collective-permute-done((bf16[2,4,3,16,128]{4,3,2,1,0:T(8,128)(2,1)S(1)}, bf16[2,4,3,16,128]{4,3,2,1,0:T(8,128)(2,1)S(1)}, u32[]{:S(2)}, u32[]{:S(2)}) %collective-permute-start.1) | collective-permute-done | bytes 98336 | tf_op jit(solution)/shard_map/ppermute | solution.py:216
  22.1 1.0 pad_maximum_fusion.1
  23.2 1.9 %collective-permute-start.2 = (bf16[2,3,14,16,128]{4,3,2,1,0:T(8,128)(2,1)S(1)}, bf16[2,3,14,16,128]{4,3,2,1,0:T(8,128)(2,1)S(1)}, u32[]{:S(2)}, u32[]{:S(2)}) collective-permute-start(bf16[2,3,14,16,128]{4,3,2,1,0:T(8,128)(2,1)S(1)} %get-tuple-element.15), channel_id=1, source_target_pairs={{0,8},{8,16},{16,24},{24,32},{32,40},{40,48},{48,56},{56,64},{64,7... | collective-permute-start | bytes 1032200 | tf_op jit(solution)/shard_map/ppermute | solution.py:216
  25.1 5.8 %collective-permute-start.3 = (bf16[2,3,14,16,128]{4,3,2,1,0:T(8,128)(2,1)S(1)}, bf16[2,3,14,16,128]{4,3,2,1,0:T(8,128)(2,1)S(1)}, u32[]{:S(2)}, u32[]{:S(2)}) collective-permute-start(bf16[2,3,14,16,128]{4,3,2,1,0:T(8,128)(2,1)S(1)} %get-tuple-element.16), channel_id=1, source_target_pairs={{8,0},{16,8},{24,16},{32,24},{40,32},{48,40},{56,48},{64,56},{72,6... | collective-permute-start | bytes 1032200 | tf_op jit(solution)/shard_map/ppermute | solution.py:216
  31.6 2.3 %collective-permute-done.2 = bf16[2,3,14,16,128]{4,3,2,1,0:T(8,128)(2,1)S(1)} collective-permute-done((bf16[2,3,14,16,128]{4,3,2,1,0:T(8,128)(2,1)S(1)}, bf16[2,3,14,16,128]{4,3,2,1,0:T(8,128)(2,1)S(1)}, u32[]{:S(2)}, u32[]{:S(2)}) %collective-permute-start.2) | collective-permute-done | bytes 344096 | tf_op jit(solution)/shard_map/ppermute | solution.py:216
  33.9 1.8 %collective-permute-done.3 = bf16[2,3,14,16,128]{4,3,2,1,0:T(8,128)(2,1)S(1)} collective-permute-done((bf16[2,3,14,16,128]{4,3,2,1,0:T(8,128)(2,1)S(1)}, bf16[2,3,14,16,128]{4,3,2,1,0:T(8,128)(2,1)S(1)}, u32[]{:S(2)}, u32[]{:S(2)}) %collective-permute-start.3) | collective-permute-done | bytes 344096 | tf_op jit(solution)/shard_map/ppermute | solution.py:216
  35.8 1.2 slice_bitcast_fusion
  37.0 12.4 %shard_map.85 = f32[10,16,128]{2,1,0:T(8,128)} custom-call(s32[3,2]{1,0:T(4,128)} %copy.10.shifts_ref, bf16[10,14,16,128]{3,2,1,0:T(8,128)(2,1)} %get-tuple-element.12.q_ref, bf16[10,14,16,128]{3,2,1,0:T(8,128)(2,1)} %get-tuple-element.11.g_ref, bf16[4,4,8,16,128]{4,3,2,1,0:T(8,128)(2,1)} %k_ref.3, bf16[4,4,8,16,128]{4,3,2,1,0:T(8,128)(2,1)} %v_ref.3, ...), custom_call_target="tpu_custom_call" | custom-call | tf_op jit(solution)/shard_map/pallas_call | solution.py:259
  50.2 1.9 %collective-permute-start.4 = (f32[3,14,128]{2,1,0:T(8,128)S(1)}, f32[3,14,128]{2,1,0:T(8,128)S(1)}, u32[]{:S(2)}, u32[]{:S(2)}) collective-permute-start(f32[3,14,128]{2,1,0:T(8,128)S(1)} %get-tuple-element.23), channel_id=1, source_target_pairs={{0,8},{8,16},{16,24},{24,32},{32,40},{40,48},{48,56},{56,64},{64,7... | collective-permute-start | bytes 64520 | tf_op jit(solution)/shard_map/ppermute | solution.py:216
  52.1 5.9 %collective-permute-start.5 = (f32[3,14,128]{2,1,0:T(8,128)S(1)}, f32[3,14,128]{2,1,0:T(8,128)S(1)}, u32[]{:S(2)}, u32[]{:S(2)}) collective-permute-start(f32[3,14,128]{2,1,0:T(8,128)S(1)} %get-tuple-element.24), channel_id=1, source_target_pairs={{8,0},{16,8},{24,16},{32,24},{40,32},{48,40},{56,48},{64,56},{72,6... | collective-permute-start | bytes 64520 | tf_op jit(solution)/shard_map/ppermute | solution.py:216
  58.1 1.5 collective-permute-done.5
  60.6 5.1 %collective-permute-start.6 = (f32[4,3,128]{2,1,0:T(4,128)S(1)}, f32[4,3,128]{2,1,0:T(4,128)S(1)}, u32[]{:S(2)}, u32[]{:S(2)}) collective-permute-start(f32[4,3,128]{2,1,0:T(4,128)S(1)} %get-tuple-element.27), channel_id=1, source_target_pairs={{0,1},{1,2},{2,3},{3,4},{4,5},{5,6},{6,7},{8,9},{9,10},{10,11},{11... | collective-permute-start | bytes 18440 | tf_op jit(solution)/shard_map/ppermute | solution.py:216
  65.7 5.6 %collective-permute-start.7 = (f32[4,3,128]{2,1,0:T(4,128)S(1)}, f32[4,3,128]{2,1,0:T(4,128)S(1)}, u32[]{:S(2)}, u32[]{:S(2)}) collective-permute-start(f32[4,3,128]{2,1,0:T(4,128)S(1)} %get-tuple-element.28), channel_id=1, source_target_pairs={{1,0},{2,1},{3,2},{4,3},{5,4},{6,5},{7,6},{9,8},{10,9},{11,10},{12... | collective-permute-start | bytes 18440 | tf_op jit(solution)/shard_map/ppermute | solution.py:216
  71.3 3.9 %collective-permute-done.7 = f32[4,3,128]{2,1,0:T(4,128)S(1)} collective-permute-done((f32[4,3,128]{2,1,0:T(4,128)S(1)}, f32[4,3,128]{2,1,0:T(4,128)S(1)}, u32[]{:S(2)}, u32[]{:S(2)}) %collective-permute-start.7) | collective-permute-done | bytes 6176 | tf_op jit(solution)/shard_map/ppermute | solution.py:216
  75.3 6.5 %collective-permute-start.8 = (f32[4,3,128]{2,1,0:T(4,128)S(1)}, f32[4,3,128]{2,1,0:T(4,128)S(1)}, u32[]{:S(2)}, u32[]{:S(2)}) collective-permute-start(f32[4,3,128]{2,1,0:T(4,128)S(1)} %get-tuple-element.31), channel_id=1, source_target_pairs={{0,1},{1,2},{2,3},{3,4},{4,5},{5,6},{6,7},{8,9},{9,10},{10,11},{11... | collective-permute-start | bytes 18440 | tf_op jit(solution)/shard_map/ppermute | solution.py:216
  81.8 4.1 %collective-permute-start.9 = (f32[4,3,128]{2,1,0:T(4,128)S(1)}, f32[4,3,128]{2,1,0:T(4,128)S(1)}, u32[]{:S(2)}, u32[]{:S(2)}) collective-permute-start(f32[4,3,128]{2,1,0:T(4,128)S(1)} %get-tuple-element.32), channel_id=1, source_target_pairs={{1,0},{2,1},{3,2},{4,3},{5,4},{6,5},{7,6},{9,8},{10,9},{11,10},{12... | collective-permute-start | bytes 18440 | tf_op jit(solution)/shard_map/ppermute | solution.py:216
  86.0 5.3 %collective-permute-done.9 = f32[4,3,128]{2,1,0:T(4,128)S(1)} collective-permute-done((f32[4,3,128]{2,1,0:T(4,128)S(1)}, f32[4,3,128]{2,1,0:T(4,128)S(1)}, u32[]{:S(2)}, u32[]{:S(2)}) %collective-permute-start.9) | collective-permute-done | bytes 6176 | tf_op jit(solution)/shard_map/ppermute | solution.py:216
  91.4 1.9 %collective-permute-start.10 = (f32[3,14,128]{2,1,0:T(8,128)S(1)}, f32[3,14,128]{2,1,0:T(8,128)S(1)}, u32[]{:S(2)}, u32[]{:S(2)}) collective-permute-start(f32[3,14,128]{2,1,0:T(8,128)S(1)} %get-tuple-element.29), channel_id=1, source_target_pairs={{0,8},{8,16},{16,24},{24,32},{32,40},{40,48},{48,56},{56,64},{64,7... | collective-permute-start | bytes 64520 | tf_op jit(solution)/shard_map/ppermute | solution.py:216
  93.3 5.8 %collective-permute-start.11 = (f32[3,14,128]{2,1,0:T(8,128)S(1)}, f32[3,14,128]{2,1,0:T(8,128)S(1)}, u32[]{:S(2)}, u32[]{:S(2)}) collective-permute-start(f32[3,14,128]{2,1,0:T(8,128)S(1)} %get-tuple-element.30), channel_id=1, source_target_pairs={{8,0},{16,8},{24,16},{32,24},{40,32},{48,40},{56,48},{64,56},{72,6... | collective-permute-start | bytes 64520 | tf_op jit(solution)/shard_map/ppermute | solution.py:216
  99.1 1.5 collective-permute-done.11
  101.3 30.5 %shard_map.86 = (f32[10,14,16,128]{3,2,1,0:T(8,128)}, bf16[4,4,8,16,128]{4,3,2,1,0:T(8,128)(2,1)}, bf16[4,4,8,16,128]{4,3,2,1,0:T(8,128)(2,1)}) custom-call(s32[3,2]{1,0:T(4,128)} %copy.10.shifts_ref, bf16[10,14,16,128]{3,2,1,0:T(8,128)(2,1)} %get-tuple-element.12.q_ref, bf16[10,14,16,128]{3,2,1,0:T(8,128)(2,1)} %get-tuple-element.11.g_ref, ...), custom_call_target="tpu_custom_call" | custom-call | tf_op jit(solution)/shard_map/pallas_call | solution.py:275
  131.8 1.3 convert.16
  133.1 1.9 %collective-permute-start.12 = (bf16[3,14,16,128]{3,2,1,0:T(8,128)(2,1)S(1)}, bf16[3,14,16,128]{3,2,1,0:T(8,128)(2,1)S(1)}, u32[]{:S(2)}, u32[]{:S(2)}) collective-permute-start(bf16[3,14,16,128]{3,2,1,0:T(8,128)(2,1)S(1)} %get-tuple-element.13), channel_id=1, source_target_pairs={{0,8},{8,16},{16,24},{24,32},{32,40},{40,48},{48,56},{56,64},{64,7... | collective-permute-start | bytes 516104 | tf_op jit(solution)/shard_map/ppermute | solution.py:216
  135.1 5.8 %collective-permute-start.13 = (bf16[3,14,16,128]{3,2,1,0:T(8,128)(2,1)S(1)}, bf16[3,14,16,128]{3,2,1,0:T(8,128)(2,1)S(1)}, u32[]{:S(2)}, u32[]{:S(2)}) collective-permute-start(bf16[3,14,16,128]{3,2,1,0:T(8,128)(2,1)S(1)} %get-tuple-element.14), channel_id=1, source_target_pairs={{8,0},{16,8},{24,16},{32,24},{40,32},{48,40},{56,48},{64,56},{72,6... | collective-permute-start | bytes 516104 | tf_op jit(solution)/shard_map/ppermute | solution.py:216
  140.8 1.1 collective-permute-done.12
  142.0 1.8 %collective-permute-done.13 = bf16[3,14,16,128]{3,2,1,0:T(8,128)(2,1)S(1)} collective-permute-done((bf16[3,14,16,128]{3,2,1,0:T(8,128)(2,1)S(1)}, bf16[3,14,16,128]{3,2,1,0:T(8,128)(2,1)S(1)}, u32[]{:S(2)}, u32[]{:S(2)}) %collective-permute-start.13) | collective-permute-done | bytes 172064 | tf_op jit(solution)/shard_map/ppermute | solution.py:216
  143.7 1.1 fusion.24
  144.8 4.8 %collective-permute-start.14 = (bf16[4,3,16,128]{3,2,1,0:T(8,128)(2,1)S(1)}, bf16[4,3,16,128]{3,2,1,0:T(8,128)(2,1)S(1)}, u32[]{:S(2)}, u32[]{:S(2)}) collective-permute-start(bf16[4,3,16,128]{3,2,1,0:T(8,128)(2,1)S(1)} %get-tuple-element.19), channel_id=1, source_target_pairs={{0,1},{1,2},{2,3},{3,4},{4,5},{5,6},{6,7},{8,9},{9,10},{10,11},{11... | collective-permute-start | bytes 147464 | tf_op jit(solution)/shard_map/ppermute | solution.py:216
  149.7 5.8 %collective-permute-start.15 = (bf16[4,3,16,128]{3,2,1,0:T(8,128)(2,1)S(1)}, bf16[4,3,16,128]{3,2,1,0:T(8,128)(2,1)S(1)}, u32[]{:S(2)}, u32[]{:S(2)}) collective-permute-start(bf16[4,3,16,128]{3,2,1,0:T(8,128)(2,1)S(1)} %get-tuple-element.20), channel_id=1, source_target_pairs={{1,0},{2,1},{3,2},{4,3},{5,4},{6,5},{7,6},{9,8},{10,9},{11,10},{12... | collective-permute-start | bytes 147464 | tf_op jit(solution)/shard_map/ppermute | solution.py:216
  156.1 4.0 %collective-permute-done.15 = bf16[4,3,16,128]{3,2,1,0:T(8,128)(2,1)S(1)} collective-permute-done((bf16[4,3,16,128]{3,2,1,0:T(8,128)(2,1)S(1)}, bf16[4,3,16,128]{3,2,1,0:T(8,128)(2,1)S(1)}, u32[]{:S(2)}, u32[]{:S(2)}) %collective-permute-start.15) | collective-permute-done | bytes 49184 | tf_op jit(solution)/shard_map/ppermute | solution.py:216
  (33 shorter events, 6.5 us)
Async XLA Ops:
  1.5 11.3 %collective-permute-start = (bf16[2,4,3,16,128]{4,3,2,1,0:T(8,128)(2,1)S(1)}, bf16[2,4,3,16,128]{4,3,2,1,0:T(8,128)(2,1)S(1)}, u32[]{:S(2)}, u32[]{:S(2)}) collective-permute-start(bf16[2,4,3,16,128]{4,3,2,1,0:T(8,128)(2,1)S(1)} %get-tuple-element.17), channel_id=1, source_target_pairs={{0,1},{1,2},{2,3},{3,4},{4,5},{5,6},{6,7},{8,9},{9,10},{10,11},{11... | collective-permute-start | bytes 294920 | tf_op jit(solution)/shard_map/ppermute | solution.py:216
  9.7 21.2 %copy-start.3 = (s32[3,2]{0,1:T(2,128)S(1)}, s32[3,2]{0,1:T(2,128)}, u32[]{:S(2)}) copy-start(s32[3,2]{0,1:T(2,128)} %param.10) | copy-start | bytes 76
  9.8 25.9 %copy-start = (bf16[4,8,16,128]{3,2,1,0:T(8,128)(2,1)S(1)}, bf16[4,8,16,128]{3,2,1,0:T(8,128)(2,1)}, u32[]{:S(2)}) copy-start(bf16[4,8,16,128]{3,2,1,0:T(8,128)(2,1)} %param.9) | copy-start | bytes 393220
  9.8 25.9 %copy-start.1 = (bf16[4,8,16,128]{3,2,1,0:T(8,128)(2,1)S(1)}, bf16[4,8,16,128]{3,2,1,0:T(8,128)(2,1)}, u32[]{:S(2)}) copy-start(bf16[4,8,16,128]{3,2,1,0:T(8,128)(2,1)} %param.6) | copy-start | bytes 393220
  9.8 12.3 %collective-permute-start.1 = (bf16[2,4,3,16,128]{4,3,2,1,0:T(8,128)(2,1)S(1)}, bf16[2,4,3,16,128]{4,3,2,1,0:T(8,128)(2,1)S(1)}, u32[]{:S(2)}, u32[]{:S(2)}) collective-permute-start(bf16[2,4,3,16,128]{4,3,2,1,0:T(8,128)(2,1)S(1)} %get-tuple-element.18), channel_id=1, source_target_pairs={{1,0},{2,1},{3,2},{4,3},{5,4},{6,5},{7,6},{9,8},{10,9},{11,10},{12... | collective-permute-start | bytes 294920 | tf_op jit(solution)/shard_map/ppermute | solution.py:216
  23.2 10.7 %collective-permute-start.2 = (bf16[2,3,14,16,128]{4,3,2,1,0:T(8,128)(2,1)S(1)}, bf16[2,3,14,16,128]{4,3,2,1,0:T(8,128)(2,1)S(1)}, u32[]{:S(2)}, u32[]{:S(2)}) collective-permute-start(bf16[2,3,14,16,128]{4,3,2,1,0:T(8,128)(2,1)S(1)} %get-tuple-element.15), channel_id=1, source_target_pairs={{0,8},{8,16},{16,24},{24,32},{32,40},{40,48},{48,56},{56,64},{64,7... | collective-permute-start | bytes 1032200 | tf_op jit(solution)/shard_map/ppermute | solution.py:216
  25.1 10.5 %collective-permute-start.3 = (bf16[2,3,14,16,128]{4,3,2,1,0:T(8,128)(2,1)S(1)}, bf16[2,3,14,16,128]{4,3,2,1,0:T(8,128)(2,1)S(1)}, u32[]{:S(2)}, u32[]{:S(2)}) collective-permute-start(bf16[2,3,14,16,128]{4,3,2,1,0:T(8,128)(2,1)S(1)} %get-tuple-element.16), channel_id=1, source_target_pairs={{8,0},{16,8},{24,16},{32,24},{40,32},{48,40},{56,48},{64,56},{72,6... | collective-permute-start | bytes 1032200 | tf_op jit(solution)/shard_map/ppermute | solution.py:216
  37.0 22.5 %copy-start.2 = (f32[128]{0:T(128)S(1)}, f32[128]{0:T(128)}, u32[]{:S(2)}) copy-start(f32[128]{0:T(128)} %constant.8.clone.1) | copy-start | bytes 1540
  50.2 7.9 %collective-permute-start.4 = (f32[3,14,128]{2,1,0:T(8,128)S(1)}, f32[3,14,128]{2,1,0:T(8,128)S(1)}, u32[]{:S(2)}, u32[]{:S(2)}) collective-permute-start(f32[3,14,128]{2,1,0:T(8,128)S(1)} %get-tuple-element.23), channel_id=1, source_target_pairs={{0,8},{8,16},{16,24},{24,32},{32,40},{40,48},{48,56},{56,64},{64,7... | collective-permute-start | bytes 64520 | tf_op jit(solution)/shard_map/ppermute | solution.py:216
  52.1 7.4 %collective-permute-start.5 = (f32[3,14,128]{2,1,0:T(8,128)S(1)}, f32[3,14,128]{2,1,0:T(8,128)S(1)}, u32[]{:S(2)}, u32[]{:S(2)}) collective-permute-start(f32[3,14,128]{2,1,0:T(8,128)S(1)} %get-tuple-element.24), channel_id=1, source_target_pairs={{8,0},{16,8},{24,16},{32,24},{40,32},{48,40},{56,48},{64,56},{72,6... | collective-permute-start | bytes 64520 | tf_op jit(solution)/shard_map/ppermute | solution.py:216
  60.6 10.7 %collective-permute-start.6 = (f32[4,3,128]{2,1,0:T(4,128)S(1)}, f32[4,3,128]{2,1,0:T(4,128)S(1)}, u32[]{:S(2)}, u32[]{:S(2)}) collective-permute-start(f32[4,3,128]{2,1,0:T(4,128)S(1)} %get-tuple-element.27), channel_id=1, source_target_pairs={{0,1},{1,2},{2,3},{3,4},{4,5},{5,6},{6,7},{8,9},{9,10},{10,11},{11... | collective-permute-start | bytes 18440 | tf_op jit(solution)/shard_map/ppermute | solution.py:216
  65.7 9.5 %collective-permute-start.7 = (f32[4,3,128]{2,1,0:T(4,128)S(1)}, f32[4,3,128]{2,1,0:T(4,128)S(1)}, u32[]{:S(2)}, u32[]{:S(2)}) collective-permute-start(f32[4,3,128]{2,1,0:T(4,128)S(1)} %get-tuple-element.28), channel_id=1, source_target_pairs={{1,0},{2,1},{3,2},{4,3},{5,4},{6,5},{7,6},{9,8},{10,9},{11,10},{12... | collective-permute-start | bytes 18440 | tf_op jit(solution)/shard_map/ppermute | solution.py:216
  75.3 10.7 %collective-permute-start.8 = (f32[4,3,128]{2,1,0:T(4,128)S(1)}, f32[4,3,128]{2,1,0:T(4,128)S(1)}, u32[]{:S(2)}, u32[]{:S(2)}) collective-permute-start(f32[4,3,128]{2,1,0:T(4,128)S(1)} %get-tuple-element.31), channel_id=1, source_target_pairs={{0,1},{1,2},{2,3},{3,4},{4,5},{5,6},{6,7},{8,9},{9,10},{10,11},{11... | collective-permute-start | bytes 18440 | tf_op jit(solution)/shard_map/ppermute | solution.py:216
  81.8 9.5 %collective-permute-start.9 = (f32[4,3,128]{2,1,0:T(4,128)S(1)}, f32[4,3,128]{2,1,0:T(4,128)S(1)}, u32[]{:S(2)}, u32[]{:S(2)}) collective-permute-start(f32[4,3,128]{2,1,0:T(4,128)S(1)} %get-tuple-element.32), channel_id=1, source_target_pairs={{1,0},{2,1},{3,2},{4,3},{5,4},{6,5},{7,6},{9,8},{10,9},{11,10},{12... | collective-permute-start | bytes 18440 | tf_op jit(solution)/shard_map/ppermute | solution.py:216
  91.4 7.7 %collective-permute-start.10 = (f32[3,14,128]{2,1,0:T(8,128)S(1)}, f32[3,14,128]{2,1,0:T(8,128)S(1)}, u32[]{:S(2)}, u32[]{:S(2)}) collective-permute-start(f32[3,14,128]{2,1,0:T(8,128)S(1)} %get-tuple-element.29), channel_id=1, source_target_pairs={{0,8},{8,16},{16,24},{24,32},{32,40},{40,48},{48,56},{56,64},{64,7... | collective-permute-start | bytes 64520 | tf_op jit(solution)/shard_map/ppermute | solution.py:216
  93.3 7.3 %collective-permute-start.11 = (f32[3,14,128]{2,1,0:T(8,128)S(1)}, f32[3,14,128]{2,1,0:T(8,128)S(1)}, u32[]{:S(2)}, u32[]{:S(2)}) collective-permute-start(f32[3,14,128]{2,1,0:T(8,128)S(1)} %get-tuple-element.30), channel_id=1, source_target_pairs={{8,0},{16,8},{24,16},{32,24},{40,32},{48,40},{56,48},{64,56},{72,6... | collective-permute-start | bytes 64520 | tf_op jit(solution)/shard_map/ppermute | solution.py:216
  133.1 8.8 %collective-permute-start.12 = (bf16[3,14,16,128]{3,2,1,0:T(8,128)(2,1)S(1)}, bf16[3,14,16,128]{3,2,1,0:T(8,128)(2,1)S(1)}, u32[]{:S(2)}, u32[]{:S(2)}) collective-permute-start(bf16[3,14,16,128]{3,2,1,0:T(8,128)(2,1)S(1)} %get-tuple-element.13), channel_id=1, source_target_pairs={{0,8},{8,16},{16,24},{24,32},{32,40},{40,48},{48,56},{56,64},{64,7... | collective-permute-start | bytes 516104 | tf_op jit(solution)/shard_map/ppermute | solution.py:216
  135.1 8.7 %collective-permute-start.13 = (bf16[3,14,16,128]{3,2,1,0:T(8,128)(2,1)S(1)}, bf16[3,14,16,128]{3,2,1,0:T(8,128)(2,1)S(1)}, u32[]{:S(2)}, u32[]{:S(2)}) collective-permute-start(bf16[3,14,16,128]{3,2,1,0:T(8,128)(2,1)S(1)} %get-tuple-element.14), channel_id=1, source_target_pairs={{8,0},{16,8},{24,16},{32,24},{40,32},{48,40},{56,48},{64,56},{72,6... | collective-permute-start | bytes 516104 | tf_op jit(solution)/shard_map/ppermute | solution.py:216
  144.8 11.3 %collective-permute-start.14 = (bf16[4,3,16,128]{3,2,1,0:T(8,128)(2,1)S(1)}, bf16[4,3,16,128]{3,2,1,0:T(8,128)(2,1)S(1)}, u32[]{:S(2)}, u32[]{:S(2)}) collective-permute-start(bf16[4,3,16,128]{3,2,1,0:T(8,128)(2,1)S(1)} %get-tuple-element.19), channel_id=1, source_target_pairs={{0,1},{1,2},{2,3},{3,4},{4,5},{5,6},{6,7},{8,9},{9,10},{10,11},{11... | collective-permute-start | bytes 147464 | tf_op jit(solution)/shard_map/ppermute | solution.py:216
  149.7 10.4 %collective-permute-start.15 = (bf16[4,3,16,128]{3,2,1,0:T(8,128)(2,1)S(1)}, bf16[4,3,16,128]{3,2,1,0:T(8,128)(2,1)S(1)}, u32[]{:S(2)}, u32[]{:S(2)}) collective-permute-start(bf16[4,3,16,128]{3,2,1,0:T(8,128)(2,1)S(1)} %get-tuple-element.20), channel_id=1, source_target_pairs={{1,0},{2,1},{3,2},{4,3},{5,4},{6,5},{7,6},{9,8},{10,9},{11,10},{12... | collective-permute-start | bytes 147464 | tf_op jit(solution)/shard_map/ppermute | solution.py:216

commit v2 on v1

v2 whole, which is shorter than its diff:
```python
import functools
import math

import jax
import jax.numpy as jnp
import numpy as np
from jax import lax
from jax.experimental import pallas as pl
from jax.experimental.pallas import tpu as pltpu
from jax.sharding import PartitionSpec as P

HEADS = 4
HD = 32
C = 128
Z = 16
FRAMES = 4
R = 3
BX = 4
BY = 8
HX = BX + 2 * R
HY = BY + 2 * R
SCALE = 1.0 / math.sqrt(HD)
C2 = SCALE * math.log2(math.e)
NEG = -1e30
KEYS_Y = ((0, 2), (0, 4), (0, 6), (2, 8), (4, 8), (6, 8))


def bias_table():
    rx = np.arange(6) - 2
    col = np.arange(4)
    cx, cy = col // 2, col % 2
    okx = np.abs(rx[:, None] - cx[None]) <= 2
    oky = np.abs(rx[:, None] - cy[None]) <= 2
    z = np.arange(Z)
    okz = np.abs(z[:, None] - z[None]) <= 1
    ok = okx[:, None, None, :, None, None] & oky[None, :, None, :, None, None]
    ok = ok & okz[None, None, :, None, None, :]
    ok = np.broadcast_to(ok, (6, 6, Z, 4, HEADS, Z)).reshape(6, 6, Z, 4 * HEADS * Z)
    return jnp.asarray(np.where(ok, 0.0, NEG).astype(np.float32))


def head_masks():
    lane = lax.broadcasted_iota(jnp.int32, (Z, C), 1) // HD
    return [jnp.where(lane == h, 1.0, 0.0).astype(jnp.bfloat16) for h in range(HEADS)]


def expanded(ref, which, x, y, masks):
    parts = []
    for cx in range(2):
        for cy in range(2):
            column = ref[which, x + cx, y + cy]
            parts += [column * mask for mask in masks]
    return jnp.concatenate(parts, 0)


def dot_t(a, b):
    return lax.dot_general(a, b, (((1,), (1,)), ((), ())), preferred_element_type=jnp.float32)


def dot_n(a, b):
    return lax.dot_general(a, b, (((1,), (0,)), ((), ())), preferred_element_type=jnp.float32)


def dot_l(a, b):
    return lax.dot_general(a, b, (((0,), (0,)), ((), ())), preferred_element_type=jnp.float32)


def low_half():
    return lax.broadcasted_iota(jnp.int32, (1, C), 1) < C // 2


def window_start(shifts_ref, f):
    past = jnp.maximum(f - 1, 0)
    ox = jnp.where(f > 0, shifts_ref[past, 0], 0)
    oy = jnp.where(f > 0, shifts_ref[past, 1], 0)
    return 1 - ox, 1 - oy


def merged(a, b):
    low = lax.broadcasted_iota(jnp.int32, a.shape, a.ndim - 1) < C // 2
    la = jnp.where(low, a, pltpu.roll(a, C // 2, a.ndim - 1))
    lb = jnp.where(low, b, pltpu.roll(b, C // 2, b.ndim - 1))
    top = jnp.maximum(la, lb)
    wa, wb = jnp.exp2(la - top), jnp.exp2(lb - top)
    total = wa + wb
    return jnp.where(low, top + jnp.log2(total), (wa * a + wb * b) / total)


class Exchange:
    def __init__(self, axis, index, sems, forward, backward):
        me, n = lax.axis_index(axis), lax.axis_size(axis)
        send, recv = sems
        self.has_next, self.has_prev = me < n - 1, me > 0
        self.forward = [
            self.copy(src, dst, send.at[index + i], recv.at[index + i], {axis: me + 1})
            for i, (src, dst) in enumerate(forward)
        ]
        index += len(forward)
        self.backward = [
            self.copy(src, dst, send.at[index + i], recv.at[index + i], {axis: me - 1})
            for i, (src, dst) in enumerate(backward)
        ]

    @staticmethod
    def copy(src, dst, send, recv, device):
        return pltpu.make_async_remote_copy(
            src_ref=src,
            dst_ref=dst,
            send_sem=send,
            recv_sem=recv,
            device_id=device,
            device_id_type=pl.DeviceIdType.MESH,
        )

    def start(self):
        @pl.when(self.has_next)
        def _():
            for c in self.forward:
                c.start()

        @pl.when(self.has_prev)
        def _():
            for c in self.backward:
                c.start()

    def wait_recv(self):
        @pl.when(self.has_prev)
        def _():
            for c in self.forward:
                c.wait_recv()

        @pl.when(self.has_next)
        def _():
            for c in self.backward:
                c.wait_recv()

    def wait_send(self):
        @pl.when(self.has_next)
        def _():
            for c in self.forward:
                c.wait_send()

        @pl.when(self.has_prev)
        def _():
            for c in self.backward:
                c.wait_send()


MID = (2, 3)
OUTER = (0, 1, 4, 5)


def kernel(
    shifts_ref, q_in, g_in, k_in, v_in, bias_in, dq_ref, dk_ref, dv_ref,
    k_ref, v_ref, bias_ref, qgx, qgy, qgh, lse_w, dn_w, sys_, syr, ownc, sxr, finx, finy, fin,
    dk_a, dv_a, dq_w, dys, dyr, own_dq, dxs, dxr, local_sem, send_sem, recv_sem,
):
    sems = (send_sem, recv_sem)
    masks = head_masks()
    low = low_half()
    head_of_lane = lax.broadcasted_iota(jnp.int32, (Z, C), 1) // HD
    loads = [
        pltpu.make_async_copy(src, dst, local_sem.at[i])
        for i, (src, dst) in enumerate(
            (
                (q_in, qgx.at[0, R : R + BX]),
                (g_in, qgx.at[1, R : R + BX]),
                (k_in, k_ref),
                (v_in, v_ref),
                (bias_in, bias_ref),
            )
        )
    ]
    for c in loads:
        c.start()

    zero16 = jnp.bfloat16(0)
    neutral = jnp.where(low, NEG, 0.0)
    for ref in (qgx.at[:, 0:R], qgx.at[:, R + BX : HX], qgy, dyr, dxr):
        ref[...] = jnp.full(ref.shape, zero16)
    for ref in (syr, sxr):
        ref[...] = jnp.broadcast_to(neutral, ref.shape)
    for ref in (finx, finy):
        ref[...] = jnp.zeros(ref.shape, jnp.float32)

    barrier = pltpu.get_barrier_semaphore()
    for axis in ("gx", "gy"):
        me, n = lax.axis_index(axis), lax.axis_size(axis)
        for there, step in ((me > 0, -1), (me < n - 1, 1)):

            @pl.when(there)
            def _():
                pl.semaphore_signal(
                    barrier, inc=1, device_id={axis: me + step}, device_id_type=pl.DeviceIdType.MESH
                )

    peers = jnp.int32(0)
    for axis in ("gx", "gy"):
        me, n = lax.axis_index(axis), lax.axis_size(axis)
        peers = peers + jnp.where(me > 0, 1, 0) + jnp.where(me < n - 1, 1, 0)
    pl.semaphore_wait(barrier, peers)

    tail = slice(BX - R, BX)
    halo_y = Exchange(
        "gy", 0, sems,
        [(q_in.at[:, BY - R : BY], qgy.at[0, 0, R : R + BX]), (g_in.at[:, BY - R : BY], qgy.at[0, 1, R : R + BX])],
        [(q_in.at[:, 0:R], qgy.at[1, 0, R : R + BX]), (g_in.at[:, 0:R], qgy.at[1, 1, R : R + BX])],
    )
    halo_x = Exchange(
        "gx", 4, sems,
        [(q_in.at[tail], qgx.at[0, 0:R]), (g_in.at[tail], qgx.at[1, 0:R])],
        [(q_in.at[0:R], qgx.at[0, R + BX : HX]), (g_in.at[0:R], qgx.at[1, R + BX : HX])],
    )
    halo_c = Exchange(
        "gx", 8, sems,
        [(qgy.at[:, :, BX : BX + R], qgy.at[:, :, 0:R])],
        [(qgy.at[:, :, R : 2 * R], qgy.at[:, :, R + BX : HX])],
    )
    stat_y = Exchange("gy", 10, sems, [(sys_.at[1], syr.at[0])], [(sys_.at[0], syr.at[1])])
    stat_x = Exchange(
        "gx", 12, sems, [(ownc.at[R + BX : HX], sxr.at[0])], [(ownc.at[0:R], sxr.at[1])]
    )
    fin_y = Exchange(
        "gy", 14, sems,
        [(finx.at[R : R + BX], finy.at[0, R : R + BX])],
        [(finx.at[R : R + BX], finy.at[1, R : R + BX])],
    )
    fin_x = Exchange(
        "gx", 16, sems,
        [(finx.at[BX : BX + R], finx.at[0:R])],
        [(finx.at[R : 2 * R], finx.at[R + BX : HX])],
    )
    fin_c = Exchange(
        "gx", 18, sems,
        [(finy.at[:, BX : BX + R], finy.at[:, 0:R])],
        [(finy.at[:, R : 2 * R], finy.at[:, R + BX : HX])],
    )
    dq_y = Exchange("gy", 20, sems, [(dys.at[1], dyr.at[0])], [(dys.at[0], dyr.at[1])])
    dq_x = Exchange("gx", 22, sems, [(dxs.at[1], dxr.at[0])], [(dxs.at[0], dxr.at[1])])

    halo_y.start()
    halo_x.start()
    lse_w[...] = jnp.full(lse_w.shape, NEG, jnp.float32)
    dn_w[...] = jnp.zeros(dn_w.shape, jnp.float32)
    dk_a[...] = jnp.zeros(dk_a.shape, jnp.float32)
    dv_a[...] = jnp.zeros(dv_a.shape, jnp.float32)
    dq_w[...] = jnp.zeros(dq_w.shape, jnp.float32)

    def part(body, bys, first, last, hook=None):
        def frame(f, carry):
            if hook is not None:
                pl.when(f == last - 1)(hook)
            sx, sy = window_start(shifts_ref, f)

            def step(j, carry):
                for by in bys:
                    body(f, sx, sy, 3 * j, 2, 2 * j, by)
                for by in bys:
                    body(f, sx, sy, 1 + j, 4, 0, by)
                return carry

            lax.fori_loop(0, 2, step, 0)
            return carry

        lax.fori_loop(first, last, frame, 0)

    def operands(f, sx, sy, bx, nx, kx0, by):
        y0, y1 = KEYS_Y[by]
        rows = nx * (y1 - y0) * Z
        xq, yq = sx + 2 * bx, sy + 2 * by
        src, yo = (qgx, yq - R) if by in MID else (qgh, yq)
        qe = expanded(src, 0, xq, yo, masks)
        ge = expanded(src, 1, xq, yo, masks)
        kt = k_ref[f, pl.ds(kx0, nx), y0:y1].reshape(rows, C)
        vt = v_ref[f, pl.ds(kx0, nx), y0:y1].reshape(rows, C)
        r0 = y0 + 4 - 2 * by
        bias = bias_ref[pl.ds(kx0 + 4 - 2 * bx, nx), r0 : r0 + y1 - y0].reshape(rows, 256)
        return qe, ge, kt, vt, bias, rows

    def stats(f, sx, sy, bx, nx, kx0, by):
        qe, ge, kt, vt, bias, rows = operands(f, sx, sy, bx, nx, kx0, by)
        t = (dot_t(kt, qe) + bias).reshape(rows // 8, 8, 256)
        ga = dot_t(vt, ge).reshape(rows // 8, 8, 256)
        m = jnp.max(t, 0)
        e = jnp.exp2((t - m[None]) * C2)
        l = jnp.sum(e, 0)
        d = jnp.sum(e * ga, 0)
        top = jnp.max(m, 0, keepdims=True)
        w = jnp.exp2((m - top) * C2)
        l = jnp.sum(l * w, 0, keepdims=True)
        d = jnp.sum(d * w, 0, keepdims=True)
        lse = top * C2 + jnp.log2(l)
        dn = d / l
        for cx in range(2):
            for val, dst in ((lse, lse_w), (dn, dn_w)):
                v2 = val[:, cx * C : (cx + 1) * C]
                other = pltpu.roll(v2, C // 2, 1)
                dst[f, 2 + 2 * bx + cx, 2 + 2 * by : 3 + 2 * by] = jnp.where(low, v2, other)
                dst[f, 2 + 2 * bx + cx, 3 + 2 * by : 4 + 2 * by] = jnp.where(low, other, v2)

    def grads(f, sx, sy, bx, nx, kx0, by):
        qe, ge, kt, vt, bias, rows = operands(f, sx, sy, bx, nx, kx0, by)
        y0, y1 = KEYS_Y[by]
        xq, yq = sx + 2 * bx, sy + 2 * by
        src, yo = (finx, yq - R) if by in MID else (fin, yq + 5)
        lses, dels = [], []
        for cx in range(2):
            a = src[xq + cx, pl.ds(yo, 1)]
            b = src[xq + cx, pl.ds(yo + 1, 1)]
            lses.append(jnp.where(low, a, pltpu.roll(b, C // 2, 1)))
            dels.append(jnp.where(low, pltpu.roll(a, C // 2, 1), b))
        lse = jnp.concatenate(lses, 1)
        delta = jnp.concatenate(dels, 1)
        att = jnp.exp2((dot_t(kt, qe) + bias) * C2 - lse)
        gs = (att * (dot_t(vt, ge) - delta)).astype(jnp.bfloat16)
        wt = att.astype(jnp.bfloat16)
        dk_a[f, pl.ds(kx0, nx), y0:y1] += dot_n(gs, qe).reshape(nx, y1 - y0, Z, C)
        dv_a[f, pl.ds(kx0, nx), y0:y1] += dot_n(wt, ge).reshape(nx, y1 - y0, Z, C)
        dq = dot_l(gs, kt)
        for cx in range(2):
            for cy in range(2):
                base = (2 * cx + cy) * HEADS * Z
                out = dq[base : base + Z]
                for h in range(1, HEADS):
                    piece = dq[base + h * Z : base + (h + 1) * Z]
                    out = jnp.where(head_of_lane == h, piece, out)
                dq_w[f, 2 + 2 * bx + cx, 2 + 2 * by + cy] = out

    def frames_merged(r):
        ls, ds = [], []
        for f in range(FRAMES):
            sx, sy = window_start(shifts_ref, f)
            ls.append(lse_w[f, r + 2 - sx, pl.ds(2 - sy, 16)])
            ds.append(dn_w[f, r + 2 - sx, pl.ds(2 - sy, 16)])
        top = functools.reduce(jnp.maximum, ls)
        ws = [jnp.exp2(x - top) for x in ls]
        total = sum(ws)
        mean = sum(w * x for w, x in zip(ws, ds)) / total
        return jnp.where(low, top + jnp.log2(total), mean)

    halo_x.wait_recv()
    for c in loads:
        c.wait()

    def forward_corners():
        halo_y.wait_recv()
        halo_c.start()

    part(stats, MID, 0, 2, forward_corners)
    halo_c.wait_recv()

    def assemble(r, carry):
        for a in range(2):
            qgh[a, r, 0:R] = qgy[0, a, r]
            qgh[a, r, R : R + BY] = qgx[a, r]
            qgh[a, r, R + BY : HY] = qgy[1, a, r]
        return carry

    lax.fori_loop(0, HX, assemble, 0)
    part(stats, OUTER, 0, 4)
    row8 = lax.broadcasted_iota(jnp.int32, (8, C), 0)

    def rims(r, carry):
        val = frames_merged(r)
        sys_[0, r] = jnp.where(row8 >= 8 - R, pltpu.roll(val[0:8], 8 - R, 0), neutral)
        sys_[1, r] = jnp.where(row8 < R, pltpu.roll(val[8:16], 8 - R, 0), neutral)
        return carry

    lax.fori_loop(0, HX, rims, 0)
    stat_y.start()
    part(stats, MID, 2, 4)
    stat_y.wait_recv()

    def core_rows(r, carry):
        ownc[r] = merged(merged(frames_merged(r)[R : R + BY], syr[0, r]), syr[1, r])
        return carry

    lax.fori_loop(0, HX, core_rows, 0)
    stat_x.start()
    stat_x.wait_recv()
    for i in range(BX):
        val = ownc[R + i]
        if i < R:
            val = merged(val, sxr[0, i])
        if i >= BX - R:
            val = merged(val, sxr[1, i - (BX - R)])
        finx[R + i] = val
    fin_y.start()
    fin_x.start()

    fin_x.wait_recv()

    def forward_stats():
        fin_y.wait_recv()
        fin_c.start()

    part(grads, MID, 0, 2, forward_stats)
    fin_c.wait_recv()
    fin[:, 0:8] = finy[0]
    fin[:, 8:16] = finx[...]
    fin[:, 16:24] = finy[1]
    part(grads, OUTER, 0, 4)

    def dq_rims(r, carry):
        for side, at in ((0, 0), (1, R + BY)):
            total = jnp.zeros((R, Z, C), jnp.float32)
            for f in range(FRAMES):
                sx, sy = window_start(shifts_ref, f)
                total = total + dq_w[f, r + 2 - sx, pl.ds(2 - sy + at, R)]
            dys[side, r] = (total * SCALE).astype(jnp.bfloat16)
        return carry

    lax.fori_loop(0, HX, dq_rims, 0)
    dq_y.start()
    part(grads, MID, 2, 4)
    dq_y.wait_recv()

    def dq_core(r, carry):
        total = jnp.zeros((BY, Z, C), jnp.float32)
        for f in range(FRAMES):
            sx, sy = window_start(shifts_ref, f)
            total = total + dq_w[f, r + 2 - sx, pl.ds(2 - sy + R, BY)]
        own_dq[r] = total * SCALE
        own_dq[r, 0:R] += dyr[0, r].astype(jnp.float32)
        own_dq[r, BY - R : BY] += dyr[1, r].astype(jnp.float32)
        return carry

    lax.fori_loop(0, HX, dq_core, 0)
    dxs[0] = own_dq[0:R].astype(jnp.bfloat16)
    dxs[1] = own_dq[R + BX : HX].astype(jnp.bfloat16)
    dq_x.start()

    def convert(f, carry):
        dk_ref[f] = (dk_a[f] * SCALE).astype(jnp.bfloat16)
        dv_ref[f] = dv_a[f].astype(jnp.bfloat16)
        return carry

    lax.fori_loop(0, FRAMES, convert, 0)
    dq_x.wait_recv()
    for i in range(BX):
        val = own_dq[R + i]
        if i < R:
            val = val + dxr[0, i].astype(jnp.float32)
        if i >= BX - R:
            val = val + dxr[1, i - (BX - R)].astype(jnp.float32)
        dq_ref[i] = val.astype(jnp.bfloat16)
    for ex in (halo_y, halo_x, halo_c, stat_y, stat_x, fin_y, fin_x, fin_c, dq_y, dq_x):
        ex.wait_send()


def per_device(saved_queries, saved_keys, saved_values, out_grad, shifts):
    bf, f32 = jnp.bfloat16, jnp.float32
    frames = saved_keys.shape
    vmem = pl.BlockSpec(memory_space=pltpu.VMEM)
    return pl.pallas_call(
        kernel,
        out_shape=(
            jax.ShapeDtypeStruct(saved_queries.shape, bf),
            jax.ShapeDtypeStruct(frames, bf),
            jax.ShapeDtypeStruct(frames, bf),
        ),
        in_specs=[pl.BlockSpec(memory_space=pltpu.SMEM)] + [pl.BlockSpec(memory_space=pl.ANY)] * 5,
        out_specs=(vmem, vmem, vmem),
        scratch_shapes=[
            pltpu.VMEM(frames, bf),
            pltpu.VMEM(frames, bf),
            pltpu.VMEM((6, 6, Z, 256), f32),
            pltpu.VMEM((2, HX, BY, Z, C), bf),
            pltpu.VMEM((2, 2, HX, R, Z, C), bf),
            pltpu.VMEM((2, HX, HY, Z, C), bf),
            pltpu.VMEM((FRAMES, 12, 24, C), f32),
            pltpu.VMEM((FRAMES, 12, 24, C), f32),
            pltpu.VMEM((2, HX, 8, C), f32),
            pltpu.VMEM((2, HX, 8, C), f32),
            pltpu.VMEM((HX, 8, C), f32),
            pltpu.VMEM((2, R, 8, C), f32),
            pltpu.VMEM((HX, 8, C), f32),
            pltpu.VMEM((2, HX, 8, C), f32),
            pltpu.VMEM((HX, 24, C), f32),
            pltpu.VMEM(frames, f32),
            pltpu.VMEM(frames, f32),
            pltpu.VMEM((FRAMES, 12, 16, Z, C), f32),
            pltpu.VMEM((2, HX, R, Z, C), bf),
            pltpu.VMEM((2, HX, R, Z, C), bf),
            pltpu.VMEM((HX, BY, Z, C), f32),
            pltpu.VMEM((2, R, BY, Z, C), bf),
            pltpu.VMEM((2, R, BY, Z, C), bf),
            pltpu.SemaphoreType.DMA((5,)),
            pltpu.SemaphoreType.DMA((24,)),
            pltpu.SemaphoreType.DMA((24,)),
        ],
        compiler_params=pltpu.CompilerParams(
            collective_id=0, has_side_effects=True, vmem_limit_bytes=60 * 2**20
        ),
    )(shifts, saved_queries, out_grad, saved_keys, saved_values, bias_table())


def solution(mesh):
    block = P("gx", "gy", None, None)
    frames = P(None, "gx", "gy", None, None)
    return jax.shard_map(
        per_device,
        mesh=mesh,
        in_specs=(block, frames, frames, block, P()),
        out_specs=(block, frames, frames),
        check_vma=False,
    )
```

time: 162 us -> 97.1 us (0.60)
  the two profiles are of different devices: /device:TPU:40 before, /device:TPU:23 now
where the time goes in v2:
time: 97.1 us; the launch traced here: 97 us
  Pallas kernels  90.7 us (93%)
  local copies, waits for them, and re-layouts  5.64 us (6%)
    pallas_call x1, Pallas kernels, per_device(): pl.pallas_call(kernel, out_shape=(jax.ShapeDtypeStruct(saved_queries.shap...  90.7 us
    unnamed x6, local copies, waits for them, and re-layouts  5.64 us

profile of v2, /device:TPU:23, one launch (start us, length us, event | category | flops | bytes accessed | tf_op | source)
XLA Modules:
  0.0 97.0 jit_solution(5793733907271484611)
XLA Ops:
  0.6 1.3 %copy.9.shifts_ref = s32[3,2]{1,0:T(4,128)} copy(s32[3,2]{0,1:T(2,128)} %param.10) | data formatting | bytes 48 | tf_op args[4]
  2.0 90.7 %shard_map.85 = (bf16[4,8,16,128]{3,2,1,0:T(8,128)(2,1)}, bf16[4,4,8,16,128]{4,3,2,1,0:T(8,128)(2,1)}, bf16[4,4,8,16,128]{4,3,2,1,0:T(8,128)(2,1)}) custom-call(s32[3,2]{1,0:T(4,128)} %copy.9.shifts_ref, bf16[4,8,16,128]{3,2,1,0:T(8,128)(2,1)} %q_in.1, bf16[4,8,16,128]{3,2,1,0:T(8,128)(2,1)} %g_in.1, bf16[4,4,8,16,128]{4,3,2,1,0:T(8,128)(2,1)} %k_in.1, ...), custom_call_target="tpu_custom_call" | custom-call | tf_op jit(solution)/shard_map/pallas_call | solution.py:455
  92.6 1.6 %copy.13 = bf16[4,8,16,128]{3,2,1,0:T(8,128)(2,1)} copy(bf16[4,8,16,128]{3,2,1,0:T(8,128)(2,1)} %get-tuple-element.6) | data formatting | bytes 262144
  94.2 0.0 copy-start
  94.2 1.9 %copy.14 = bf16[4,4,8,16,128]{4,3,2,1,0:T(8,128)(2,1)} copy(bf16[4,4,8,16,128]{4,3,2,1,0:T(8,128)(2,1)} %get-tuple-element.7) | data formatting | bytes 1048576
  96.2 0.0 copy-done
  96.2 0.8 copy.15
Async XLA Ops:
  94.2 1.9 %copy-start = (bf16[4,4,8,16,128]{4,3,2,1,0:T(8,128)(2,1)S(1)}, bf16[4,4,8,16,128]{4,3,2,1,0:T(8,128)(2,1)}, u32[]{:S(2)}) copy-start(bf16[4,4,8,16,128]{4,3,2,1,0:T(8,128)(2,1)} %get-tuple-element.8) | copy-start | bytes 1572868

commit v3 on v2

v3 whole, which is shorter than its diff:
```python
import functools
import math

import jax
import jax.numpy as jnp
import numpy as np
from jax import lax
from jax.experimental import pallas as pl
from jax.experimental.pallas import tpu as pltpu
from jax.sharding import PartitionSpec as P

HEADS = 4
HD = 32
C = 128
Z = 16
FRAMES = 4
R = 3
BX = 4
BY = 8
HX = BX + 2 * R
HY = BY + 2 * R
SCALE = 1.0 / math.sqrt(HD)
C2 = SCALE * math.log2(math.e)
NEG = -1e30
KEYS_Y = ((0, 2), (0, 4), (0, 6), (2, 8), (4, 8), (6, 8))


def bias_table():
    rx = np.arange(6) - 2
    col = np.arange(4)
    cx, cy = col // 2, col % 2
    okx = np.abs(rx[:, None] - cx[None]) <= 2
    oky = np.abs(rx[:, None] - cy[None]) <= 2
    z = np.arange(Z)
    okz = np.abs(z[:, None] - z[None]) <= 1
    ok = okx[:, None, None, :, None, None] & oky[None, :, None, :, None, None]
    ok = ok & okz[None, None, :, None, None, :]
    ok = np.broadcast_to(ok, (6, 6, Z, 4, HEADS, Z)).reshape(6, 6, Z, 4 * HEADS * Z)
    return jnp.asarray(np.where(ok, 0.0, NEG).astype(np.float32))


def head_masks():
    lane = lax.broadcasted_iota(jnp.int32, (Z, C), 1) // HD
    return [jnp.where(lane == h, 1.0, 0.0).astype(jnp.bfloat16) for h in range(HEADS)]


def expanded(ref, which, x, y, masks):
    parts = []
    for cx in range(2):
        for cy in range(2):
            column = ref[which, x + cx, y + cy]
            parts += [column * mask for mask in masks]
    return jnp.concatenate(parts, 0)


def dot_t(a, b):
    return lax.dot_general(a, b, (((1,), (1,)), ((), ())), preferred_element_type=jnp.float32)


def dot_n(a, b):
    return lax.dot_general(a, b, (((1,), (0,)), ((), ())), preferred_element_type=jnp.float32)


def dot_l(a, b):
    return lax.dot_general(a, b, (((0,), (0,)), ((), ())), preferred_element_type=jnp.float32)


def low_half():
    return lax.broadcasted_iota(jnp.int32, (1, C), 1) < C // 2


def window_start(shifts_ref, f):
    past = jnp.maximum(f - 1, 0)
    ox = jnp.where(f > 0, shifts_ref[past, 0], 0)
    oy = jnp.where(f > 0, shifts_ref[past, 1], 0)
    return 1 - ox, 1 - oy


def merged(a, b):
    low = lax.broadcasted_iota(jnp.int32, a.shape, a.ndim - 1) < C // 2
    la = jnp.where(low, a, pltpu.roll(a, C // 2, a.ndim - 1))
    lb = jnp.where(low, b, pltpu.roll(b, C // 2, b.ndim - 1))
    top = jnp.maximum(la, lb)
    wa, wb = jnp.exp2(la - top), jnp.exp2(lb - top)
    total = wa + wb
    return jnp.where(low, top + jnp.log2(total), (wa * a + wb * b) / total)


class Message:
    def __init__(self, offset, src, dst, index, sems):
        device, self.has_target, self.has_source = {}, True, True
        for axis, by in offset.items():
            at, n = lax.axis_index(axis), lax.axis_size(axis)
            device[axis] = at + by
            to, back = at + by, at - by
            self.has_target = self.has_target & (to >= 0) & (to < n)
            self.has_source = self.has_source & (back >= 0) & (back < n)
        self.copy = pltpu.make_async_remote_copy(
            src_ref=src,
            dst_ref=dst,
            send_sem=sems[0].at[index],
            recv_sem=sems[1].at[index],
            device_id=device,
            device_id_type=pl.DeviceIdType.MESH,
        )

    def start(self):
        pl.when(self.has_target)(self.copy.start)

    def wait_recv(self):
        pl.when(self.has_source)(self.copy.wait_recv)

    def wait_send(self):
        pl.when(self.has_target)(self.copy.wait_send)


PEERS = tuple(
    [{"gx": d} for d in (-2, -1, 1, 2)]
    + [{"gy": d} for d in (-1, 1)]
    + [{"gx": dx, "gy": dy} for dx in (-1, 1) for dy in (-1, 1)]
)
MID = (2, 3)
OUTER = (0, 1, 4, 5)
NROWS = [2 * Z * (b - a) for a, b in KEYS_Y]
FIRST_ROW = {2: [sum(NROWS[:i]) for i in range(6)]}
FIRST_ROW[4] = [sum(NROWS) + 2 * v for v in FIRST_ROW[2]]
ROWS = 3 * sum(NROWS)
MESSAGES = 32


def kernel(
    shifts_in, q_in, g_in, k_in, v_in, bias_in, dq_out, dk_out, dv_out,
    shifts_ref, k_ref, v_ref, bias_ref, qgx, qgy, qgh, lse_w, dn_w, part_s, ry, rx1, rx2, fin,
    e_s, ga_s, m_s, dk_a, dv_a, dq_w, dys, dyr, dcr, own_dq, dxs, dxr, dq_v,
    local_sem, out_sem, send_sem, recv_sem,
):
    sems = (send_sem, recv_sem)
    masks = head_masks()
    low = low_half()
    head_of_lane = lax.broadcasted_iota(jnp.int32, (Z, C), 1) // HD
    loads = [
        pltpu.make_async_copy(src, dst, local_sem.at[i])
        for i, (src, dst) in enumerate(
            (
                (shifts_in, shifts_ref),
                (q_in, qgx.at[0, R : R + BX]),
                (g_in, qgx.at[1, R : R + BX]),
                (k_in, k_ref),
                (v_in, v_ref),
                (bias_in, bias_ref),
            )
        )
    ]
    for c in loads:
        c.start()

    zero16 = jnp.bfloat16(0)
    neutral = jnp.where(low, NEG, 0.0)
    for ref in (qgx.at[:, 0:R], qgx.at[:, R + BX : HX], qgy, dyr, dcr, dxr):
        ref[...] = jnp.full(ref.shape, zero16)
    for ref in (ry, rx1, rx2):
        ref[...] = jnp.broadcast_to(neutral, ref.shape)

    barrier = pltpu.get_barrier_semaphore()
    count = jnp.int32(0)
    for offset in PEERS:
        there = True
        for axis, by in offset.items():
            to = lax.axis_index(axis) + by
            there = there & (to >= 0) & (to < lax.axis_size(axis))
        device = {axis: lax.axis_index(axis) + by for axis, by in offset.items()}
        count = count + jnp.where(there, 1, 0)

        @pl.when(there)
        def _():
            pl.semaphore_signal(barrier, inc=1, device_id=device, device_id_type=pl.DeviceIdType.MESH)

    pl.semaphore_wait(barrier, count)

    made = []

    def message(offset, src, dst):
        made.append(Message(offset, src, dst, len(made), sems))
        return made[-1]

    up, down, right, left = {"gy": 1}, {"gy": -1}, {"gx": 1}, {"gx": -1}
    tail = slice(BX - R, BX)
    own = slice(R, R + BX)
    past = slice(R + BX, HX)
    halo_y, halo_x = [], []
    for i, ref in enumerate((q_in, g_in)):
        halo_y.append(message(up, ref.at[:, BY - R : BY], qgy.at[0, i, own]))
        halo_y.append(message(down, ref.at[:, 0:R], qgy.at[1, i, own]))
        halo_x.append(message(right, ref.at[tail], qgx.at[i, 0:R]))
        halo_x.append(message(left, ref.at[0:R], qgx.at[i, past]))
    halo_c = [
        message(right, qgy.at[:, :, BX : BX + R], qgy.at[:, :, 0:R]),
        message(left, qgy.at[:, :, R : 2 * R], qgy.at[:, :, past]),
    ]
    stat_y = [
        message(up, part_s.at[0, :, 8:16], ry.at[0]),
        message(down, part_s.at[0, :, 0:8], ry.at[1]),
    ]
    stat_x = [
        message(right, part_s.at[1, 4:10], rx1.at[0]),
        message(left, part_s.at[1, 0:6], rx1.at[1]),
        message({"gx": 2}, part_s.at[1, 8:10], rx2.at[0]),
        message({"gx": -2}, part_s.at[1, 0:2], rx2.at[1]),
    ]
    dq_far = [
        message(up, dys.at[1, own], dyr.at[0]),
        message(down, dys.at[0, own], dyr.at[1]),
    ]
    for xs, dx, rows in ((0, 1, past), (1, -1, slice(0, R))):
        for ys, dy, side in ((0, 1, 1), (1, -1, 0)):
            dq_far.append(message({"gx": dx, "gy": dy}, dys.at[side, rows], dcr.at[xs, ys]))
    dq_near = [message(right, dxs.at[1], dxr.at[0]), message(left, dxs.at[0], dxr.at[1])]

    for m in halo_y + halo_x:
        m.start()
    lse_w[...] = jnp.full(lse_w.shape, NEG, jnp.float32)
    dn_w[...] = jnp.zeros(dn_w.shape, jnp.float32)
    dk_a[...] = jnp.zeros(dk_a.shape, jnp.float32)
    dv_a[...] = jnp.zeros(dv_a.shape, jnp.float32)
    dq_w[:, :, 0:2] = jnp.zeros((FRAMES, 8, 2, Z, C), jnp.float32)
    dq_w[:, :, 14:16] = jnp.zeros((FRAMES, 8, 2, Z, C), jnp.float32)

    def part(body, bys, hook=None):
        def frame(f, carry):
            if hook is not None:
                pl.when(f == FRAMES - 1)(hook)
            sx, sy = window_start(shifts_ref, f)

            def step(j, carry):
                for by in bys:
                    body(f, j, sx, sy, 3 * j, 2, 2 * j, by)
                for by in bys:
                    body(f, j, sx, sy, 1 + j, 4, 0, by)
                return carry

            lax.fori_loop(0, 2, step, 0)
            return carry

        lax.fori_loop(0, FRAMES, frame, 0)

    def place(nx, by):
        y0, y1 = KEYS_Y[by]
        rows = nx * (y1 - y0) * Z
        return y0, y1, rows, slice(FIRST_ROW[nx][by], FIRST_ROW[nx][by] + rows), by + (nx // 4) * 6

    def stats(f, j, sx, sy, bx, nx, kx0, by):
        y0, y1, rows, at, slot = place(nx, by)
        xq, yq = sx + 2 * bx, sy + 2 * by
        src, yo = (qgx, yq - R) if by in MID else (qgh, yq)
        qe = expanded(src, 0, xq, yo, masks)
        ge = expanded(src, 1, xq, yo, masks)
        kt = k_ref[f, pl.ds(kx0, nx), y0:y1].reshape(rows, C)
        vt = v_ref[f, pl.ds(kx0, nx), y0:y1].reshape(rows, C)
        r0 = y0 + 4 - 2 * by
        bias = bias_ref[pl.ds(kx0 + 4 - 2 * bx, nx), r0 : r0 + y1 - y0].reshape(rows, 256)
        t = (dot_t(kt, qe) + bias).reshape(rows // 8, 8, 256)
        ga = dot_t(vt, ge)
        ga_s[2 * f + j, at] = ga
        ga = ga.reshape(rows // 8, 8, 256)
        m = jnp.max(t, 0)
        m_s[2 * f + j, slot] = m
        e = jnp.exp2((t - m[None]) * C2)
        e_s[2 * f + j, at] = e.reshape(rows, 256).astype(jnp.bfloat16)
        l = jnp.sum(e, 0)
        d = jnp.sum(e * ga, 0)
        top = jnp.max(m, 0, keepdims=True)
        w = jnp.exp2((m - top) * C2)
        l = jnp.sum(l * w, 0, keepdims=True)
        d = jnp.sum(d * w, 0, keepdims=True)
        lse = top * C2 + jnp.log2(l)
        dn = d / l
        for cx in range(2):
            for val, dst in ((lse, lse_w), (dn, dn_w)):
                v2 = val[:, cx * C : (cx + 1) * C]
                other = pltpu.roll(v2, C // 2, 1)
                dst[f, 2 + 2 * bx + cx, 2 + 2 * by : 3 + 2 * by] = jnp.where(low, v2, other)
                dst[f, 2 + 2 * bx + cx, 3 + 2 * by : 4 + 2 * by] = jnp.where(low, other, v2)

    def grads(f, j, sx, sy, bx, nx, kx0, by):
        y0, y1, rows, at, slot = place(nx, by)
        xq, yq = sx + 2 * bx, sy + 2 * by
        lses, dels = [], []
        for cx in range(2):
            a = fin[xq + cx, pl.ds(yq, 1)]
            b = fin[xq + cx, pl.ds(yq + 1, 1)]
            lses.append(jnp.where(low, a, pltpu.roll(b, C // 2, 1)))
            dels.append(jnp.where(low, pltpu.roll(a, C // 2, 1), b))
        lse = jnp.concatenate(lses, 1)
        delta = jnp.concatenate(dels, 1)
        level = jnp.exp2(m_s[2 * f + j, slot] * C2 - lse)
        e = e_s[2 * f + j, at].astype(jnp.float32).reshape(rows // 8, 8, 256)
        att = (e * level[None]).reshape(rows, 256)
        gs = (att * (ga_s[2 * f + j, at] - delta)).astype(jnp.bfloat16)
        wt = att.astype(jnp.bfloat16)
        qe = expanded(qgh, 0, xq, yq, masks)
        ge = expanded(qgh, 1, xq, yq, masks)
        kt = k_ref[f, pl.ds(kx0, nx), y0:y1].reshape(rows, C)
        dk_a[f, pl.ds(kx0, nx), y0:y1] += dot_n(gs, qe).reshape(nx, y1 - y0, Z, C)
        dv_a[f, pl.ds(kx0, nx), y0:y1] += dot_n(wt, ge).reshape(nx, y1 - y0, Z, C)
        dq = dot_l(kt, gs).T
        for cx in range(2):
            for cy in range(2):
                base = (2 * cx + cy) * HEADS * Z
                out = dq[base : base + Z]
                for h in range(1, HEADS):
                    piece = dq[base + h * Z : base + (h + 1) * Z]
                    out = jnp.where(head_of_lane == h, piece, out)
                dq_w[f, 2 * bx + cx, 2 + 2 * by + cy] = out

    def frames_merged(r):
        ls, ds = [], []
        for f in range(FRAMES):
            sx, sy = window_start(shifts_ref, f)
            ls.append(lse_w[f, r + 2 - sx, pl.ds(2 - sy, 16)])
            ds.append(dn_w[f, r + 2 - sx, pl.ds(2 - sy, 16)])
        top = functools.reduce(jnp.maximum, ls)
        ws = [jnp.exp2(x - top) for x in ls]
        total = sum(ws)
        mean = sum(w * x for w, x in zip(ws, ds)) / total
        return jnp.where(low, top + jnp.log2(total), mean)

    for m in halo_x:
        m.wait_recv()
    for c in loads:
        c.wait()

    def forward_corners():
        for m in halo_y:
            m.wait_recv()
        for m in halo_c:
            m.start()

    part(stats, MID, forward_corners)
    for m in halo_c:
        m.wait_recv()

    def assemble(r, carry):
        for a in range(2):
            qgh[a, r, 0:R] = qgy[0, a, r]
            qgh[a, r, R : R + BY] = qgx[a, r]
            qgh[a, r, R + BY : HY] = qgy[1, a, r]
        return carry

    lax.fori_loop(0, HX, assemble, 0)
    part(stats, OUTER)

    def partial_rows(r, carry):
        part_s[0, r] = frames_merged(r)
        return carry

    lax.fori_loop(0, HX, partial_rows, 0)
    for m in stat_y:
        m.start()
    for m in stat_y:
        m.wait_recv()
    part_s[1, :, 0:8] = merged(part_s[0, :, 0:8], ry[0])
    part_s[1, :, 8:16] = merged(part_s[0, :, 8:16], ry[1])
    for m in stat_x:
        m.start()
    for m in stat_x:
        m.wait_recv()
    for r in range(HX):
        val = part_s[1, r]
        if r < 6:
            val = merged(val, rx1[0, r])
        if r >= 4:
            val = merged(val, rx1[1, r - 4])
        if r < 2:
            val = merged(val, rx2[0, r])
        if r >= 8:
            val = merged(val, rx2[1, r - 8])
        fin[r] = val

    part(grads, OUTER)

    def dq_sum(r, at, n):
        total = jnp.zeros((n, Z, C), jnp.float32)
        for f in range(FRAMES):
            sx, sy = window_start(shifts_ref, f)
            w = r - sx
            row = dq_w[f, jnp.clip(w, 0, 7), pl.ds(2 - sy + at, n)]
            total = total + jnp.where((w >= 0) & (w < 8), row, 0.0)
        return total * SCALE

    def dq_rims(r, carry):
        dys[0, r] = dq_sum(r, 0, R).astype(jnp.bfloat16)
        dys[1, r] = dq_sum(r, R + BY, R).astype(jnp.bfloat16)
        return carry

    lax.fori_loop(0, HX, dq_rims, 0)
    for m in dq_far:
        m.start()
    part(grads, MID)

    def dq_sides(i, carry):
        dxs[0, i] = dq_sum(i, R, BY).astype(jnp.bfloat16)
        dxs[1, i] = dq_sum(i + R + BX, R, BY).astype(jnp.bfloat16)
        return carry

    lax.fori_loop(0, R, dq_sides, 0)
    for m in dq_near:
        m.start()

    def convert(f, carry):
        k_ref[f] = (dk_a[f] * SCALE).astype(jnp.bfloat16)
        v_ref[f] = dv_a[f].astype(jnp.bfloat16)
        return carry

    lax.fori_loop(0, FRAMES, convert, 0)
    stores = [
        pltpu.make_async_copy(src, dst, out_sem.at[i])
        for i, (src, dst) in enumerate(((k_ref, dk_out), (v_ref, dv_out), (dq_v, dq_out)))
    ]
    stores[0].start()
    stores[1].start()

    def dq_core(i, carry):
        own_dq[i] = dq_sum(i + R, R, BY)
        return carry

    lax.fori_loop(0, BX, dq_core, 0)
    for m in dq_far + dq_near:
        m.wait_recv()
    rims = (slice(0, R), slice(BY - R, BY))
    for i in range(BX):
        for xs, ok, at in ((0, i < R, i), (1, i >= BX - R, i - (BX - R))):
            if ok:
                own_dq[i] += dxr[xs, at].astype(jnp.float32)
                for ys in range(2):
                    own_dq[i, rims[ys]] += dcr[xs, ys, at].astype(jnp.float32)
        for ys in range(2):
            own_dq[i, rims[ys]] += dyr[ys, i].astype(jnp.float32)
    dq_v[...] = own_dq[...].astype(jnp.bfloat16)
    stores[2].start()
    for m in made:
        m.wait_send()
    for c in stores:
        c.wait()


def per_device(saved_queries, saved_keys, saved_values, out_grad, shifts):
    bf, f32 = jnp.bfloat16, jnp.float32
    frames = saved_keys.shape
    anywhere = pl.BlockSpec(memory_space=pl.ANY)
    return pl.pallas_call(
        kernel,
        out_shape=(
            jax.ShapeDtypeStruct(saved_queries.shape, bf),
            jax.ShapeDtypeStruct(frames, bf),
            jax.ShapeDtypeStruct(frames, bf),
        ),
        in_specs=[anywhere] * 6,
        out_specs=(anywhere,) * 3,
        scratch_shapes=[
            pltpu.SMEM(shifts.shape, jnp.int32),
            pltpu.VMEM(frames, bf),
            pltpu.VMEM(frames, bf),
            pltpu.VMEM((6, 6, Z, 256), f32),
            pltpu.VMEM((2, HX, BY, Z, C), bf),
            pltpu.VMEM((2, 2, HX, R, Z, C), bf),
            pltpu.VMEM((2, HX, HY, Z, C), bf),
            pltpu.VMEM((FRAMES, 12, 24, C), f32),
            pltpu.VMEM((FRAMES, 12, 24, C), f32),
            pltpu.VMEM((2, HX, 16, C), f32),
            pltpu.VMEM((2, HX, 8, C), f32),
            pltpu.VMEM((2, 6, 16, C), f32),
            pltpu.VMEM((2, 2, 16, C), f32),
            pltpu.VMEM((HX, 16, C), f32),
            pltpu.VMEM((2 * FRAMES, ROWS, 256), bf),
            pltpu.VMEM((2 * FRAMES, ROWS, 256), f32),
            pltpu.VMEM((2 * FRAMES, 12, 8, 256), f32),
            pltpu.VMEM(frames, f32),
            pltpu.VMEM(frames, f32),
            pltpu.VMEM((FRAMES, 8, 16, Z, C), f32),
            pltpu.VMEM((2, HX, R, Z, C), bf),
            pltpu.VMEM((2, BX, R, Z, C), bf),
            pltpu.VMEM((2, 2, R, R, Z, C), bf),
            pltpu.VMEM((BX, BY, Z, C), f32),
            pltpu.VMEM((2, R, BY, Z, C), bf),
            pltpu.VMEM((2, R, BY, Z, C), bf),
            pltpu.VMEM((BX, BY, Z, C), bf),
            pltpu.SemaphoreType.DMA((6,)),
            pltpu.SemaphoreType.DMA((3,)),
            pltpu.SemaphoreType.DMA((MESSAGES,)),
            pltpu.SemaphoreType.DMA((MESSAGES,)),
        ],
        compiler_params=pltpu.CompilerParams(
            collective_id=0, has_side_effects=True, vmem_limit_bytes=60 * 2**20
        ),
    )(shifts, saved_queries, out_grad, saved_keys, saved_values, bias_table())


def solution(mesh):
    block = P("gx", "gy", None, None)
    frames = P(None, "gx", "gy", None, None)
    return jax.shard_map(
        per_device,
        mesh=mesh,
        in_specs=(block, frames, frames, block, P()),
        out_specs=(block, frames, frames),
        check_vma=False,
    )
```

time: 97.1 us -> 75.9 us (0.78)
  the two profiles are of different devices: /device:TPU:23 before, /device:TPU:40 now
where the time goes in v3:
time: 75.9 us; the launch traced here: 75.8 us
  Pallas kernels  69.5 us (92%)
  local copies, waits for them, and re-layouts  5.64 us (7%)
    pallas_call x1, Pallas kernels, per_device(): pl.pallas_call(kernel, out_shape=(jax.ShapeDtypeStruct(saved_queries.shap...  69.5 us
    unnamed x6, local copies, waits for them, and re-layouts  5.64 us

profile of v3, /device:TPU:40, one launch (start us, length us, event | category | flops | bytes accessed | tf_op | source)
XLA Modules:
  0.0 75.8 jit_solution(16029838473854007954)
XLA Ops:
  0.6 1.3 %copy.9.shifts_in = s32[3,2]{1,0:T(4,128)} copy(s32[3,2]{0,1:T(2,128)} %param.10) | data formatting | bytes 48 | tf_op args[4]
  2.0 69.5 %shard_map.85 = (bf16[4,8,16,128]{3,2,1,0:T(8,128)(2,1)}, bf16[4,4,8,16,128]{4,3,2,1,0:T(8,128)(2,1)}, bf16[4,4,8,16,128]{4,3,2,1,0:T(8,128)(2,1)}) custom-call(s32[3,2]{1,0:T(4,128)} %copy.9.shifts_in, bf16[4,8,16,128]{3,2,1,0:T(8,128)(2,1)} %q_in.1, bf16[4,8,16,128]{3,2,1,0:T(8,128)(2,1)} %g_in.1, bf16[4,4,8,16,128]{4,3,2,1,0:T(8,128)(2,1)} %k_in.1, ...), custom_call_target="tpu_custom_call" | custom-call | tf_op jit(solution)/shard_map/pallas_call | solution.py:450
  71.5 1.6 %copy.13 = bf16[4,8,16,128]{3,2,1,0:T(8,128)(2,1)} copy(bf16[4,8,16,128]{3,2,1,0:T(8,128)(2,1)} %get-tuple-element.6) | data formatting | bytes 262144
  73.1 0.0 copy-start
  73.1 1.9 %copy.14 = bf16[4,4,8,16,128]{4,3,2,1,0:T(8,128)(2,1)} copy(bf16[4,4,8,16,128]{4,3,2,1,0:T(8,128)(2,1)} %get-tuple-element.7) | data formatting | bytes 1048576
  75.0 0.0 copy-done
  75.0 0.8 %copy.15 = bf16[4,4,8,16,128]{4,3,2,1,0:T(8,128)(2,1)} copy(bf16[4,4,8,16,128]{4,3,2,1,0:T(8,128)(2,1)S(1)} %copy-done) | data formatting | bytes 1048576
Async XLA Ops:
  73.1 1.9 %copy-start = (bf16[4,4,8,16,128]{4,3,2,1,0:T(8,128)(2,1)S(1)}, bf16[4,4,8,16,128]{4,3,2,1,0:T(8,128)(2,1)}, u32[]{:S(2)}) copy-start(bf16[4,4,8,16,128]{4,3,2,1,0:T(8,128)(2,1)} %get-tuple-element.8) | copy-start | bytes 1572868

commit v4 on v3

--- a/solution.py
+++ b/solution.py
@@ -71,8 +71,8 @@
 
 def window_start(shifts_ref, f):
     past = jnp.maximum(f - 1, 0)
-    ox = jnp.where(f > 0, shifts_ref[past, 0], 0)
-    oy = jnp.where(f > 0, shifts_ref[past, 1], 0)
+    ox = jnp.where(f > 0, shifts_ref[0, past], 0)
+    oy = jnp.where(f > 0, shifts_ref[1, past], 0)
     return 1 - ox, 1 - oy
 
 
@@ -120,17 +120,21 @@
     + [{"gx": dx, "gy": dy} for dx in (-1, 1) for dy in (-1, 1)]
 )
 MID = (2, 3)
-OUTER = (0, 1, 4, 5)
+LOW = (0, 1)
+HIGH = (4, 5)
+RIM = 2 * R
 NROWS = [2 * Z * (b - a) for a, b in KEYS_Y]
 FIRST_ROW = {2: [sum(NROWS[:i]) for i in range(6)]}
 FIRST_ROW[4] = [sum(NROWS) + 2 * v for v in FIRST_ROW[2]]
 ROWS = 3 * sum(NROWS)
+CHUNK = 64
+HIGH_HOOK = 2
 MESSAGES = 32
 
 
 def kernel(
     shifts_in, q_in, g_in, k_in, v_in, bias_in, dq_out, dk_out, dv_out,
-    shifts_ref, k_ref, v_ref, bias_ref, qgx, qgy, qgh, lse_w, dn_w, part_s, ry, rx1, rx2, fin,
+    shifts_ref, k_ref, v_ref, bias_ref, qgx, qgy, qgl, qgr, lse_w, dn_w, part_s, ry, rx1, rx2, fin,
     e_s, ga_s, m_s, dk_a, dv_a, dq_w, dys, dyr, dcr, own_dq, dxs, dxr, dq_v,
     local_sem, out_sem, send_sem, recv_sem,
 ):
@@ -187,15 +191,18 @@
     tail = slice(BX - R, BX)
     own = slice(R, R + BX)
     past = slice(R + BX, HX)
-    halo_y, halo_x = [], []
+    halo_lo, halo_x, halo_hi = [], [], []
     for i, ref in enumerate((q_in, g_in)):
-        halo_y.append(message(up, ref.at[:, BY - R : BY], qgy.at[0, i, own]))
-        halo_y.append(message(down, ref.at[:, 0:R], qgy.at[1, i, own]))
+        halo_lo.append(message(up, ref.at[:, BY - R : BY], qgy.at[0, i, own]))
+        halo_hi.append(message(down, ref.at[:, 0:R], qgy.at[1, i, own]))
         halo_x.append(message(right, ref.at[tail], qgx.at[i, 0:R]))
         halo_x.append(message(left, ref.at[0:R], qgx.at[i, past]))
     halo_c = [
-        message(right, qgy.at[:, :, BX : BX + R], qgy.at[:, :, 0:R]),
-        message(left, qgy.at[:, :, R : 2 * R], qgy.at[:, :, past]),
+        [
+            message(right, qgy.at[side, :, BX : BX + R], qgy.at[side, :, 0:R]),
+            message(left, qgy.at[side, :, R : 2 * R], qgy.at[side, :, past]),
+        ]
+        for side in range(2)
     ]
     stat_y = [
         message(up, part_s.at[0, :, 8:16], ry.at[0]),
@@ -207,16 +214,19 @@
         message({"gx": 2}, part_s.at[1, 8:10], rx2.at[0]),
         message({"gx": -2}, part_s.at[1, 0:2], rx2.at[1]),
     ]
-    dq_far = [
-        message(up, dys.at[1, own], dyr.at[0]),
-        message(down, dys.at[0, own], dyr.at[1]),
-    ]
-    for xs, dx, rows in ((0, 1, past), (1, -1, slice(0, R))):
-        for ys, dy, side in ((0, 1, 1), (1, -1, 0)):
-            dq_far.append(message({"gx": dx, "gy": dy}, dys.at[side, rows], dcr.at[xs, ys]))
+    dq_far = []
+    for side, dy in ((0, -1), (1, 1)):
+        ys = 1 - side
+        dq_far.append(
+            [
+                message({"gy": dy}, dys.at[side, own], dyr.at[ys]),
+                message({"gx": 1, "gy": dy}, dys.at[side, past], dcr.at[0, ys]),
+                message({"gx": -1, "gy": dy}, dys.at[side, 0:R], dcr.at[1, ys]),
+            ]
+        )
     dq_near = [message(right, dxs.at[1], dxr.at[0]), message(left, dxs.at[0], dxr.at[1])]
 
-    for m in halo_y + halo_x:
+    for m in halo_lo + halo_x + halo_hi:
         m.start()
     lse_w[...] = jnp.full(lse_w.shape, NEG, jnp.float32)
     dn_w[...] = jnp.zeros(dn_w.shape, jnp.float32)
@@ -225,53 +235,60 @@
     dq_w[:, :, 0:2] = jnp.zeros((FRAMES, 8, 2, Z, C), jnp.float32)
     dq_w[:, :, 14:16] = jnp.zeros((FRAMES, 8, 2, Z, C), jnp.float32)
 
-    def part(body, bys, hook=None):
+    def part(body, bys, hook=None, hook_frame=FRAMES - 1):
         def frame(f, carry):
             if hook is not None:
-                pl.when(f == FRAMES - 1)(hook)
+                pl.when(f == hook_frame)(hook)
             sx, sy = window_start(shifts_ref, f)
 
-            def step(j, carry):
-                for by in bys:
+            for by in bys:
+                for j in range(2):
                     body(f, j, sx, sy, 3 * j, 2, 2 * j, by)
-                for by in bys:
                     body(f, j, sx, sy, 1 + j, 4, 0, by)
-                return carry
-
-            lax.fori_loop(0, 2, step, 0)
             return carry
 
-        lax.fori_loop(0, FRAMES, frame, 0)
+        lax.fori_loop(0, FRAMES, frame, 0, unroll=2)
 
     def place(nx, by):
         y0, y1 = KEYS_Y[by]
         rows = nx * (y1 - y0) * Z
-        return y0, y1, rows, slice(FIRST_ROW[nx][by], FIRST_ROW[nx][by] + rows), by + (nx // 4) * 6
+        return y0, y1, rows, slice(FIRST_ROW[nx][by], FIRST_ROW[nx][by] + rows)
+
+    def operands(xq, yq, by):
+        if by in MID:
+            src, yo = qgx, yq - R
+        elif by in LOW:
+            src, yo = qgl, yq
+        else:
+            src, yo = qgr, yq - BY
+        return expanded(src, 0, xq, yo, masks), expanded(src, 1, xq, yo, masks)
 
     def stats(f, j, sx, sy, bx, nx, kx0, by):
-        y0, y1, rows, at, slot = place(nx, by)
+        y0, y1, rows, at = place(nx, by)
         xq, yq = sx + 2 * bx, sy + 2 * by
-        src, yo = (qgx, yq - R) if by in MID else (qgh, yq)
-        qe = expanded(src, 0, xq, yo, masks)
-        ge = expanded(src, 1, xq, yo, masks)
+        qe, ge = operands(xq, yq, by)
         kt = k_ref[f, pl.ds(kx0, nx), y0:y1].reshape(rows, C)
         vt = v_ref[f, pl.ds(kx0, nx), y0:y1].reshape(rows, C)
         r0 = y0 + 4 - 2 * by
         bias = bias_ref[pl.ds(kx0 + 4 - 2 * bx, nx), r0 : r0 + y1 - y0].reshape(rows, 256)
-        t = (dot_t(kt, qe) + bias).reshape(rows // 8, 8, 256)
+        t = (dot_t(kt, qe) + bias).reshape(rows // CHUNK, CHUNK // 8, 8, 256)
         ga = dot_t(vt, ge)
         ga_s[2 * f + j, at] = ga
-        ga = ga.reshape(rows // 8, 8, 256)
-        m = jnp.max(t, 0)
-        m_s[2 * f + j, slot] = m
-        e = jnp.exp2((t - m[None]) * C2)
-        e_s[2 * f + j, at] = e.reshape(rows, 256).astype(jnp.bfloat16)
-        l = jnp.sum(e, 0)
-        d = jnp.sum(e * ga, 0)
-        top = jnp.max(m, 0, keepdims=True)
-        w = jnp.exp2((m - top) * C2)
-        l = jnp.sum(l * w, 0, keepdims=True)
-        d = jnp.sum(d * w, 0, keepdims=True)
+        ga = ga.reshape(rows // CHUNK, CHUNK // 8, 8, 256)
+        ms, ls, ds = [], [], []
+        for i in range(rows // CHUNK):
+            m = jnp.max(t[i], 0)
+            e = jnp.exp2((t[i] - m[None]) * C2)
+            lo = at.start + i * CHUNK
+            e_s[2 * f + j, lo : lo + CHUNK] = e.reshape(CHUNK, 256).astype(jnp.bfloat16)
+            m_s[2 * f + j, lo // CHUNK] = m
+            ms.append(m)
+            ls.append(jnp.sum(e, 0))
+            ds.append(jnp.sum(e * ga[i], 0))
+        top = jnp.max(functools.reduce(jnp.maximum, ms), 0, keepdims=True)
+        ws = [jnp.exp2((m - top) * C2) for m in ms]
+        l = jnp.sum(sum(w * x for w, x in zip(ws, ls)), 0, keepdims=True)
+        d = jnp.sum(sum(w * x for w, x in zip(ws, ds)), 0, keepdims=True)
         lse = top * C2 + jnp.log2(l)
         dn = d / l
         for cx in range(2):
@@ -282,7 +299,7 @@
                 dst[f, 2 + 2 * bx + cx, 3 + 2 * by : 4 + 2 * by] = jnp.where(low, other, v2)
 
     def grads(f, j, sx, sy, bx, nx, kx0, by):
-        y0, y1, rows, at, slot = place(nx, by)
+        y0, y1, rows, at = place(nx, by)
         xq, yq = sx + 2 * bx, sy + 2 * by
         lses, dels = [], []
         for cx in range(2):
@@ -292,13 +309,13 @@
             dels.append(jnp.where(low, pltpu.roll(a, C // 2, 1), b))
         lse = jnp.concatenate(lses, 1)
         delta = jnp.concatenate(dels, 1)
-        level = jnp.exp2(m_s[2 * f + j, slot] * C2 - lse)
-        e = e_s[2 * f + j, at].astype(jnp.float32).reshape(rows // 8, 8, 256)
-        att = (e * level[None]).reshape(rows, 256)
+        n = rows // CHUNK
+        level = jnp.exp2(m_s[2 * f + j, at.start // CHUNK : at.start // CHUNK + n] * C2 - lse)
+        e = e_s[2 * f + j, at].astype(jnp.float32).reshape(n, CHUNK // 8, 8, 256)
+        att = (e * level[:, None]).reshape(rows, 256)
         gs = (att * (ga_s[2 * f + j, at] - delta)).astype(jnp.bfloat16)
         wt = att.astype(jnp.bfloat16)
-        qe = expanded(qgh, 0, xq, yq, masks)
-        ge = expanded(qgh, 1, xq, yq, masks)
+        qe, ge = operands(xq, yq, by)
         kt = k_ref[f, pl.ds(kx0, nx), y0:y1].reshape(rows, C)
         dk_a[f, pl.ds(kx0, nx), y0:y1] += dot_n(gs, qe).reshape(nx, y1 - y0, Z, C)
         dv_a[f, pl.ds(kx0, nx), y0:y1] += dot_n(wt, ge).reshape(nx, y1 - y0, Z, C)
@@ -312,12 +329,12 @@
                     out = jnp.where(head_of_lane == h, piece, out)
                 dq_w[f, 2 * bx + cx, 2 + 2 * by + cy] = out
 
-    def frames_merged(r):
+    def frames_merged(r, half):
         ls, ds = [], []
         for f in range(FRAMES):
             sx, sy = window_start(shifts_ref, f)
-            ls.append(lse_w[f, r + 2 - sx, pl.ds(2 - sy, 16)])
-            ds.append(dn_w[f, r + 2 - sx, pl.ds(2 - sy, 16)])
+            ls.append(lse_w[f, r + 2 - sx, pl.ds(2 - sy + half.start, 8)])
+            ds.append(dn_w[f, r + 2 - sx, pl.ds(2 - sy + half.start, 8)])
         top = functools.reduce(jnp.maximum, ls)
         ws = [jnp.exp2(x - top) for x in ls]
         total = sum(ws)
@@ -329,33 +346,44 @@
     for c in loads:
         c.wait()
 
-    def forward_corners():
-        for m in halo_y:
+    def corners(side):
+        for m in (halo_lo, halo_hi)[side]:
             m.wait_recv()
-        for m in halo_c:
+        for m in halo_c[side]:
             m.start()
 
-    part(stats, MID, forward_corners)
-    for m in halo_c:
-        m.wait_recv()
-
-    def assemble(r, carry):
-        for a in range(2):
-            qgh[a, r, 0:R] = qgy[0, a, r]
-            qgh[a, r, R : R + BY] = qgx[a, r]
-            qgh[a, r, R + BY : HY] = qgy[1, a, r]
-        return carry
-
-    lax.fori_loop(0, HX, assemble, 0)
-    part(stats, OUTER)
-
-    def partial_rows(r, carry):
-        part_s[0, r] = frames_merged(r)
-        return carry
-
-    lax.fori_loop(0, HX, partial_rows, 0)
-    for m in stat_y:
-        m.start()
+    def assembled(side):
+        for m in halo_c[side]:
+            m.wait_recv()
+
+        def row(r, carry):
+            for a in range(2):
+                if side == 0:
+                    qgl[a, r, 0:R] = qgy[0, a, r]
+                    qgl[a, r, R:RIM] = qgx[a, r, 0:R]
+                else:
+                    qgr[a, r, 0:R] = qgx[a, r, BY - R : BY]
+                    qgr[a, r, R:RIM] = qgy[1, a, r]
+            return carry
+
+        lax.fori_loop(0, HX, row, 0)
+
+    def partial_rows(half):
+        def row(r, carry):
+            part_s[0, r, half] = frames_merged(r, half)
+            return carry
+
+        lax.fori_loop(0, HX, row, 0)
+
+    part(stats, MID, functools.partial(corners, 0))
+    assembled(0)
+    part(stats, LOW, functools.partial(corners, 1), HIGH_HOOK)
+    partial_rows(slice(0, 8))
+    stat_y[1].start()
+    assembled(1)
+    part(stats, HIGH)
+    partial_rows(slice(8, 16))
+    stat_y[0].start()
     for m in stat_y:
         m.wait_recv()
     part_s[1, :, 0:8] = merged(part_s[0, :, 0:8], ry[0])
@@ -376,7 +404,6 @@
             val = merged(val, rx2[1, r - 8])
         fin[r] = val
 
-    part(grads, OUTER)
 
     def dq_sum(r, at, n):
         total = jnp.zeros((n, Z, C), jnp.float32)
@@ -387,14 +414,19 @@
             total = total + jnp.where((w >= 0) & (w < 8), row, 0.0)
         return total * SCALE
 
-    def dq_rims(r, carry):
-        dys[0, r] = dq_sum(r, 0, R).astype(jnp.bfloat16)
-        dys[1, r] = dq_sum(r, R + BY, R).astype(jnp.bfloat16)
-        return carry
-
-    lax.fori_loop(0, HX, dq_rims, 0)
-    for m in dq_far:
-        m.start()
+    def dq_rim(side):
+        def row(r, carry):
+            dys[side, r] = dq_sum(r, side * (R + BY), R).astype(jnp.bfloat16)
+            return carry
+
+        lax.fori_loop(0, HX, row, 0)
+        for m in dq_far[side]:
+            m.start()
+
+    part(grads, LOW)
+    dq_rim(0)
+    part(grads, HIGH)
+    dq_rim(1)
     part(grads, MID)
 
     def dq_sides(i, carry):
@@ -424,7 +456,7 @@
         return carry
 
     lax.fori_loop(0, BX, dq_core, 0)
-    for m in dq_far + dq_near:
+    for m in dq_far[0] + dq_far[1] + dq_near:
         m.wait_recv()
     rims = (slice(0, R), slice(BY - R, BY))
     for i in range(BX):
@@ -457,13 +489,14 @@
         in_specs=[anywhere] * 6,
         out_specs=(anywhere,) * 3,
         scratch_shapes=[
-            pltpu.SMEM(shifts.shape, jnp.int32),
+            pltpu.SMEM(shifts.shape[::-1], jnp.int32),
             pltpu.VMEM(frames, bf),
             pltpu.VMEM(frames, bf),
             pltpu.VMEM((6, 6, Z, 256), f32),
             pltpu.VMEM((2, HX, BY, Z, C), bf),
             pltpu.VMEM((2, 2, HX, R, Z, C), bf),
-            pltpu.VMEM((2, HX, HY, Z, C), bf),
+            pltpu.VMEM((2, HX, RIM, Z, C), bf),
+            pltpu.VMEM((2, HX, RIM, Z, C), bf),
             pltpu.VMEM((FRAMES, 12, 24, C), f32),
             pltpu.VMEM((FRAMES, 12, 24, C), f32),
             pltpu.VMEM((2, HX, 16, C), f32),
@@ -473,7 +506,7 @@
             pltpu.VMEM((HX, 16, C), f32),
             pltpu.VMEM((2 * FRAMES, ROWS, 256), bf),
             pltpu.VMEM((2 * FRAMES, ROWS, 256), f32),
-            pltpu.VMEM((2 * FRAMES, 12, 8, 256), f32),
+            pltpu.VMEM((2 * FRAMES, ROWS // CHUNK, 8, 256), f32),
             pltpu.VMEM(frames, f32),
             pltpu.VMEM(frames, f32),
             pltpu.VMEM((FRAMES, 8, 16, Z, C), f32),
@@ -492,7 +525,7 @@
         compiler_params=pltpu.CompilerParams(
             collective_id=0, has_side_effects=True, vmem_limit_bytes=60 * 2**20
         ),
-    )(shifts, saved_queries, out_grad, saved_keys, saved_values, bias_table())
+    )(shifts.T, saved_queries, out_grad, saved_keys, saved_values, bias_table())
 
 
 def solution(mesh):

time: 75.9 us -> 68.9 us (0.908)
  the two profiles are of different devices: /device:TPU:40 before, /device:TPU:29 now
where the time goes in v4:
time: 68.9 us; the launch traced here: 68.8 us
  Pallas kernels  63.8 us (93%)
  local copies, waits for them, and re-layouts  4.31 us (6%)
    pallas_call x1, Pallas kernels, per_device(): pl.pallas_call(kernel, out_shape=(jax.ShapeDtypeStruct(saved_queries.shap...  63.8 us
    unnamed x5, local copies, waits for them, and re-layouts  4.31 us

profile of v4, /device:TPU:29, one launch (start us, length us, event | category | flops | bytes accessed | tf_op | source)
XLA Modules:
  0.0 68.8 jit_solution(9131610022912022001)
XLA Ops:
  0.6 63.8 %shard_map.85 = (bf16[4,8,16,128]{3,2,1,0:T(8,128)(2,1)}, bf16[4,4,8,16,128]{4,3,2,1,0:T(8,128)(2,1)}, bf16[4,4,8,16,128]{4,3,2,1,0:T(8,128)(2,1)}) custom-call(s32[2,3]{1,0:T(2,128)} %bitcast.1, bf16[4,8,16,128]{3,2,1,0:T(8,128)(2,1)} %q_in.1, bf16[4,8,16,128]{3,2,1,0:T(8,128)(2,1)} %g_in.1, bf16[4,4,8,16,128]{4,3,2,1,0:T(8,128)(2,1)} %k_in.1, ...), custom_call_target="tpu_custom_call" | custom-call | tf_op jit(solution)/shard_map/pallas_call | solution.py:482
  64.5 1.6 %copy.12 = bf16[4,8,16,128]{3,2,1,0:T(8,128)(2,1)} copy(bf16[4,8,16,128]{3,2,1,0:T(8,128)(2,1)} %get-tuple-element.6) | data formatting | bytes 262144
  66.0 0.0 copy-start
  66.0 1.9 %copy.13 = bf16[4,4,8,16,128]{4,3,2,1,0:T(8,128)(2,1)} copy(bf16[4,4,8,16,128]{4,3,2,1,0:T(8,128)(2,1)} %get-tuple-element.7) | data formatting | bytes 1048576
  68.0 0.0 copy-done
  68.0 0.8 %copy.14 = bf16[4,4,8,16,128]{4,3,2,1,0:T(8,128)(2,1)} copy(bf16[4,4,8,16,128]{4,3,2,1,0:T(8,128)(2,1)S(1)} %copy-done) | data formatting | bytes 1048576
Async XLA Ops:
  66.0 1.9 %copy-start = (bf16[4,4,8,16,128]{4,3,2,1,0:T(8,128)(2,1)S(1)}, bf16[4,4,8,16,128]{4,3,2,1,0:T(8,128)(2,1)}, u32[]{:S(2)}) copy-start(bf16[4,4,8,16,128]{4,3,2,1,0:T(8,128)(2,1)} %get-tuple-element.8) | copy-start | bytes 1572868

commit v5 on v4

--- a/solution.py
+++ b/solution.py
@@ -128,7 +128,7 @@
 FIRST_ROW[4] = [sum(NROWS) + 2 * v for v in FIRST_ROW[2]]
 ROWS = 3 * sum(NROWS)
 CHUNK = 64
-HIGH_HOOK = 2
+HIGH_HOOK = 0
 MESSAGES = 32
 
 
@@ -226,7 +226,7 @@
         )
     dq_near = [message(right, dxs.at[1], dxr.at[0]), message(left, dxs.at[0], dxr.at[1])]
 
-    for m in halo_lo + halo_x + halo_hi:
+    for m in halo_x + halo_lo + halo_hi:
         m.start()
     lse_w[...] = jnp.full(lse_w.shape, NEG, jnp.float32)
     dn_w[...] = jnp.zeros(dn_w.shape, jnp.float32)
@@ -475,11 +475,17 @@
         c.wait()
 
 
+def hand_on(dq_in, dk_in, dv_in, dq_out, dk_out, dv_out):
+    dq_out[...] = dq_in[...]
+    dk_out[...] = dk_in[...]
+    dv_out[...] = dv_in[...]
+
+
 def per_device(saved_queries, saved_keys, saved_values, out_grad, shifts):
     bf, f32 = jnp.bfloat16, jnp.float32
     frames = saved_keys.shape
     anywhere = pl.BlockSpec(memory_space=pl.ANY)
-    return pl.pallas_call(
+    results = pl.pallas_call(
         kernel,
         out_shape=(
             jax.ShapeDtypeStruct(saved_queries.shape, bf),
@@ -526,6 +532,15 @@
             collective_id=0, has_side_effects=True, vmem_limit_bytes=60 * 2**20
         ),
     )(shifts.T, saved_queries, out_grad, saved_keys, saved_values, bias_table())
+    block = pl.BlockSpec((1,) + saved_queries.shape[1:], lambda i: (i, 0, 0, 0))
+    frame = pl.BlockSpec((1,) + frames[1:], lambda i: (i, 0, 0, 0, 0))
+    return pl.pallas_call(
+        hand_on,
+        out_shape=tuple(jax.ShapeDtypeStruct(r.shape, r.dtype) for r in results),
+        grid=(FRAMES,),
+        in_specs=[block, frame, frame],
+        out_specs=(block, frame, frame),
+    )(*results)
 
 
 def solution(mesh):

time: 68.9 us -> 61.9 us (0.90)
  the two profiles are of different devices: /device:TPU:29 before, /device:TPU:55 now
where the time goes in v5:
time: 61.9 us; the launch traced here: 61.8 us
  Pallas kernels  61.2 us (99%)
  between operations  0.64 us (1%)
    pallas_call x1, Pallas kernels, per_device(): pl.pallas_call(kernel, out_shape=(jax.ShapeDtypeStruct(saved_queries.shap...  57.7 us
    pallas_call x1, Pallas kernels, per_device(): pl.pallas_call(hand_on, out_shape=tuple((jax.ShapeDtypeStruct(r.shape, r....  3.48 us

profile of v5, /device:TPU:55, one launch (start us, length us, event | category | flops | bytes accessed | tf_op | source)
XLA Modules:
  0.0 61.8 jit_solution(8412117894341353296)
XLA Ops:
  0.6 57.7 %shard_map.85 = (bf16[4,8,16,128]{3,2,1,0:T(8,128)(2,1)}, bf16[4,4,8,16,128]{4,3,2,1,0:T(8,128)(2,1)}, bf16[4,4,8,16,128]{4,3,2,1,0:T(8,128)(2,1)}) custom-call(s32[2,3]{1,0:T(2,128)} %bitcast.1, bf16[4,8,16,128]{3,2,1,0:T(8,128)(2,1)} %q_in.1, bf16[4,8,16,128]{3,2,1,0:T(8,128)(2,1)} %g_in.1, bf16[4,4,8,16,128]{4,3,2,1,0:T(8,128)(2,1)} %k_in.1, ...), custom_call_target="tpu_custom_call" | custom-call | tf_op jit(solution)/shard_map/pallas_call | solution.py:488
  58.3 3.5 %shard_map.86 = (bf16[4,8,16,128]{3,2,1,0:T(8,128)(2,1)}, bf16[4,4,8,16,128]{4,3,2,1,0:T(8,128)(2,1)}, bf16[4,4,8,16,128]{4,3,2,1,0:T(8,128)(2,1)}) custom-call(bf16[4,8,16,128]{3,2,1,0:T(8,128)(2,1)} %get-tuple-element.6.dq_in, bf16[4,4,8,16,128]{4,3,2,1,0:T(8,128)(2,1)} %get-tuple-element.7.dk_in, bf16[4,4,8,16,128]{4,3,2,1,0:T(8,128)(2,1)} %get-tuple-element.8.dv_in), custom_call_target="tpu_custom_call" | custom-call | tf_op jit(solution)/shard_map/pallas_call | solution.py:537

commit v6 on v5

--- a/solution.py
+++ b/solution.py
@@ -375,9 +375,11 @@
 
         lax.fori_loop(0, HX, row, 0)
 
-    part(stats, MID, functools.partial(corners, 0))
+    part(stats, MID)
+    corners(0)
+    corners(1)
     assembled(0)
-    part(stats, LOW, functools.partial(corners, 1), HIGH_HOOK)
+    part(stats, LOW)
     partial_rows(slice(0, 8))
     stat_y[1].start()
     assembled(1)

time: 61.9 us -> 61.6 us (level)
  the two profiles are of different devices: /device:TPU:55 before, /device:TPU:56 now
where the time goes in v6:
time: 61.6 us; the launch traced here: 61.4 us
  Pallas kernels  60.7 us (99%)
  between operations  0.64 us (1%)
    pallas_call x1, Pallas kernels, per_device(): pl.pallas_call(kernel, out_shape=(jax.ShapeDtypeStruct(saved_queries.shap...  57.2 us
    pallas_call x1, Pallas kernels, per_device(): pl.pallas_call(hand_on, out_shape=tuple((jax.ShapeDtypeStruct(r.shape, r....  3.48 us

profile of v6, /device:TPU:56, one launch (start us, length us, event | category | flops | bytes accessed | tf_op | source)
XLA Modules:
  0.0 61.4 jit_solution(6043178759454085452)
XLA Ops:
  0.6 57.2 %shard_map.85 = (bf16[4,8,16,128]{3,2,1,0:T(8,128)(2,1)}, bf16[4,4,8,16,128]{4,3,2,1,0:T(8,128)(2,1)}, bf16[4,4,8,16,128]{4,3,2,1,0:T(8,128)(2,1)}) custom-call(s32[2,3]{1,0:T(2,128)} %bitcast.1, bf16[4,8,16,128]{3,2,1,0:T(8,128)(2,1)} %q_in.1, bf16[4,8,16,128]{3,2,1,0:T(8,128)(2,1)} %g_in.1, bf16[4,4,8,16,128]{4,3,2,1,0:T(8,128)(2,1)} %k_in.1, ...), custom_call_target="tpu_custom_call" | custom-call | tf_op jit(solution)/shard_map/pallas_call | solution.py:490
  57.9 3.5 %shard_map.86 = (bf16[4,8,16,128]{3,2,1,0:T(8,128)(2,1)}, bf16[4,4,8,16,128]{4,3,2,1,0:T(8,128)(2,1)}, bf16[4,4,8,16,128]{4,3,2,1,0:T(8,128)(2,1)}) custom-call(bf16[4,8,16,128]{3,2,1,0:T(8,128)(2,1)} %get-tuple-element.6.dq_in, bf16[4,4,8,16,128]{4,3,2,1,0:T(8,128)(2,1)} %get-tuple-element.7.dk_in, bf16[4,4,8,16,128]{4,3,2,1,0:T(8,128)(2,1)} %get-tuple-element.8.dv_in), custom_call_target="tpu_custom_call" | custom-call | tf_op jit(solution)/shard_map/pallas_call | solution.py:539
